TPU v7x, 128 devices: a whole 4x4x4 slice. The times are simulated.
128 devices in a mesh: depth: 4 (over z_lo, core), inw: 8 (over z_hi, x), outw: 4 (over y).
Axes of the slice: x: 4, y: 4, z: 4 (z_hi: 2, z_lo: 2; z = z_hi * 2 + z_lo), core: 2. Of those that a mesh axis runs over, the one named last changes fastest.
Arguments:
- inputs: bfloat16 [1536, 8192], P(('depth', 'inw'), 'outw'), may hold values from -6 to 6
- w_gate: bfloat16 [8192, 14336], P(('outw', 'depth'), 'inw'), may hold values from -0.0625 to 0.0625
- w_up: bfloat16 [8192, 14336], P(('outw', 'depth'), 'inw'), may hold values from -0.0625 to 0.0625
- w_down: bfloat16 [14336, 8192], P('inw', ('outw', 'depth')), may hold values from -0.046875 to 0.046875
- cotangent: bfloat16 [1536, 8192], P(('depth', 'inw'), 'outw'), may hold values from -1.5 to 1.5
Outputs:
- outputs: bfloat16 [1536, 8192], P(('depth', 'inw'), 'outw')
- grad_inputs: bfloat16 [1536, 8192], P(('depth', 'inw'), 'outw')
- grad_gate: bfloat16 [8192, 14336], P(('outw', 'depth'), 'inw')
- grad_up: bfloat16 [8192, 14336], P(('outw', 'depth'), 'inw')
- grad_down: bfloat16 [14336, 8192], P('inw', ('outw', 'depth'))
All inputs are finite; a program needn't handle non-finite values.
Results may differ from a plain program's by a relative error of at most 0.027.
Values may be sent and summed in bfloat16 or wider, within the bound.
No kernel may reach another device: no remote copies, remote signals or barrier semaphores. Data moves between devices by JAX's collectives and lax.ppermute only.
A program may use at most 128 MiB of HBM per device.

v0:
```python
import jax
import jax.numpy as jnp
from jax import lax
from jax.sharding import PartitionSpec as P

BF16, F32 = jnp.bfloat16, jnp.float32
STREAMS = 3
ORDERS = (("a", "b", "z"), ("b", "z", "a"), ("z", "a", "b"))


def dot(left, right, dims):
    return lax.dot_general(left, right, (dims, ((), ())), preferred_element_type=F32).astype(BF16)


def swap(value, axis, size, flip):
    return lax.ppermute(value, axis, [(i, i ^ flip) for i in range(size)])


def swap_core(value):
    return swap(value, "depth", 4, 1)


def swap_zlo(value):
    return swap(value, "depth", 4, 2)


def swap_zhi(value):
    return swap(value, "inw", 8, 4)


def swap_zboth(value):
    return lax.ppermute(value, ("depth", "inw"), [(i, i ^ 0b10100) for i in range(32)])


def swap_x(value, flip):
    return swap(value, "inw", 8, flip)


def swap_link(value, link):
    if link == "z":
        return swap_zlo(value)
    return swap(value, "outw", 4, 1 if link == "a" else 3)


def add(*terms):
    total = terms[0].astype(F32)
    for term in terms[1:]:
        total = total + term.astype(F32)
    return total


def either(bit, if_zero, if_one):
    return jnp.where(bit == 0, if_zero, if_one)


def ordered(bit, own, other, axis):
    return either(bit, jnp.concatenate([own, other], axis), jnp.concatenate([other, own], axis))


def half(value, index):
    size = value.shape[0] // 2
    return lax.dynamic_slice_in_dim(value, index * size, size, 0)


def together(*values):
    return lax.optimization_barrier(values)


def after(value, *others):
    marks = [
        lax.slice(array, [0] * array.ndim, [1] * array.ndim)
        for array in jax.tree.leaves(lax.optimization_barrier(others))
    ]
    return lax.optimization_barrier((value, marks))[0]


def reduce_give(parts, link, bits):
    return jnp.stack([half(part, 1 - bits[link]) for part in parts])


def reduce_take(parts, received, link, bits):
    return [add(half(part, bits[link]), received[i]) for i, part in enumerate(parts)]


def rounded(parts):
    return [part.astype(BF16) for part in parts]


def doubled(value, received, link, bits):
    return ordered(bits[link], value, received, 1)


def near_gives(local, zlo, core):
    rows = local.reshape(STREAMS, 16, 2048)

    def columns(z, c):
        return lax.dynamic_slice_in_dim(rows, (z * 2 + c) * 512, 512, 2)

    keep = jnp.concatenate([columns(zlo, core), columns(zlo, 1 - core)], 2)
    give = jnp.concatenate([columns(1 - zlo, core), columns(1 - zlo, 1 - core)], 2)
    return together(keep, give)


def near_send(keep, give):
    return together(swap_zlo(give), swap_zhi(keep), swap_zboth(give))


def near_gathered(keep, received, zlo):
    from_lo, from_hi, from_both = received
    return jnp.concatenate([ordered(zlo, keep, from_lo, 1), ordered(zlo, from_hi, from_both, 1)], 1)


def x_send(to_first, to_third):
    return together(swap_x(to_first, 1), swap_x(to_third, 3))


def relays(first, third):
    return together(third[:, :32], first[:, 32:])


def scatter_relays(part, received):
    to_third, to_first = received
    first = jnp.concatenate([part[:, 64:96], add(part[:, 96:128], to_first).astype(BF16)], 1)
    third = jnp.concatenate([add(part[:, 128:160], to_third).astype(BF16), part[:, 160:192]], 1)
    return together(first, third)


def scatter_near(own, zlo):
    near, far = own[:, :32], own[:, 32:]

    def rows_of(value, z):
        return lax.dynamic_slice_in_dim(value, z * 16, 16, 1)

    return rows_of(near, zlo), together(rows_of(near, 1 - zlo), rows_of(far, zlo), rows_of(far, 1 - zlo))


def scatter_send(to_lo, to_hi, to_both):
    return together(swap_zlo(to_lo), swap_zhi(to_hi), swap_zboth(to_both))


def scattered(mine, got, zlo, core):
    from_lo, from_hi, from_both = got
    mine = add(mine, from_hi).astype(BF16)
    other = add(from_lo, from_both).astype(BF16)

    def unswapped(value):
        return ordered(core, value[:, :, :512], value[:, :, 512:], 2)

    return ordered(zlo, unswapped(mine), unswapped(other), 2).reshape(-1, 2048)


def act_grads(grad_hidden, gate_sum, up_sum):
    sigmoid_gate = jax.nn.sigmoid(gate_sum)
    grad_gate_act = (
        grad_hidden * up_sum * sigmoid_gate * (1.0 + gate_sum * (1.0 - sigmoid_gate))
    ).astype(BF16)
    grad_up_act = (grad_hidden * gate_sum * sigmoid_gate).astype(BF16)
    return jnp.stack([grad_gate_act, grad_up_act])


def body(inputs, w_gate, w_up, w_down, cotangent):
    depth, outw = lax.axis_index("depth"), lax.axis_index("outw")
    zlo, core = depth >> 1, depth & 1
    bits = {"a": (outw & 1) ^ (outw >> 1), "b": outw >> 1, "z": zlo}
    streams = range(STREAMS)

    x_keep, x_give = near_gives(inputs, zlo, core)
    gate_got, up_got, x_got, cot = together(
        swap_core(w_gate), swap_core(w_up), near_send(x_keep, x_give), cotangent
    )
    x_near = near_gathered(x_keep, x_got, zlo)
    cot_keep, cot_give = near_gives(cot, zlo, core)
    x_first, cot_got, gate, up = together(
        x_send(x_near, x_near),
        near_send(cot_keep, cot_give),
        jnp.concatenate([w_gate, gate_got], 0),
        jnp.concatenate([w_up, up_got], 0),
    )
    x_second, cot_near, down_got = together(
        x_send(*relays(*x_first)), near_gathered(cot_keep, cot_got, zlo), swap_core(w_down)
    )
    x_all = jnp.concatenate([x_near, *x_first, *x_second], 1)

    s_parts = [[dot(x_all[s], gate, ((1,), (0,))), dot(x_all[s], up, ((1,), (0,)))] for s in streams]
    s_gives = [reduce_give(s_parts[s], ORDERS[s][0], bits) for s in streams]
    cot_first = x_send(cot_near, cot_near)
    cot_first, down = together(after(cot_first, s_gives), jnp.concatenate([w_down, down_got], 1))
    cot_all = jnp.concatenate([cot_near, *cot_first, *x_send(*relays(*cot_first))], 1)
    g_parts = [[dot(cot_all[s], down, ((1,), (1,)))] for s in streams]

    hidden, acts, act_gots = [], [], []
    for s in streams:
        links = ORDERS[s]
        s_part, g_part, s_give = s_parts[s], g_parts[s], s_gives[s]
        g_give = reduce_give(g_part, links[0], bits)
        s_part = rounded(reduce_take(s_part, swap_link(s_give, links[0]), links[0], bits))
        s_give = reduce_give(s_part, links[1], bits)
        g_got, s_part = together(swap_link(g_give, links[0]), s_part)
        g_part = rounded(reduce_take(g_part, g_got, links[0], bits))
        g_give = reduce_give(g_part, links[1], bits)
        s_got, g_part = together(swap_link(s_give, links[1]), g_part)
        s_give = jnp.stack(rounded(reduce_take(s_part, s_got, links[1], bits)))
        g_got, s_part = together(swap_link(g_give, links[1]), s_give)
        g_give = rounded(reduce_take(g_part, g_got, links[1], bits))[0]
        s_got, g_part = together(swap_link(s_give, links[2]), g_give)
        gate_sum, up_sum = add(s_part, s_got)
        hid = (jax.nn.silu(gate_sum) * up_sum).astype(BF16)[None]
        grad_hidden = add(g_part, after(swap_link(g_give, links[2]), hid))
        act = act_grads(grad_hidden, gate_sum, up_sum)
        hid = doubled(hid, swap_link(hid, links[1]), links[1], bits)
        act = doubled(act, swap_link(act, links[1]), links[1], bits)
        hidden.append(doubled(hid, swap_link(hid, links[0]), links[0], bits)[0])
        acts.append(act)
        act_gots.append(swap_link(act, links[0]))
    out_part = jnp.stack([dot(h, down, ((1,), (0,))) for h in hidden])
    hidden_all = jnp.concatenate(hidden, 0)
    cot_rows = cot_all.reshape(768, 1024)
    down_other = dot(hidden_all, cot_rows[:, 512:], ((0,), (0,)))
    act_gots, out_got, down_other = together(
        act_gots, x_send(out_part[:, 192:224], out_part[:, 224:256]), down_other
    )

    acts = [doubled(acts[s], act_gots[s], ORDERS[s][0], bits) for s in streams]

    def input_term(act):
        left = lax.dot_general(act[0], gate, (((1,), (1,)), ((), ())), preferred_element_type=F32)
        right = lax.dot_general(act[1], up, (((1,), (1,)), ((), ())), preferred_element_type=F32)
        return (left + right).astype(BF16)

    def own_plus(left, right, got):
        return add(lax.dot_general(left, right, (((0,), (0,)), ((), ())), preferred_element_type=F32), got).astype(BF16)

    in_part = jnp.stack([input_term(act) for act in acts])
    in_second = in_part[:, 192:]
    out_relays = scatter_relays(out_part, out_got)
    x_rows = x_all.reshape(768, 1024)
    act_gate = jnp.concatenate([act[0] for act in acts], 0)
    act_up = jnp.concatenate([act[1] for act in acts], 0)
    gate_other = dot(x_rows[:, 512:], act_gate, ((0,), (0,)))
    out_got = x_send(*out_relays)
    in_got, out_got, down_got, gate_other = together(
        x_send(in_second[:, :32], in_second[:, 32:]), out_got, swap_core(down_other), gate_other
    )
    in_relays = scatter_relays(in_part, in_got)
    up_other = dot(x_rows[:, 512:], act_up, ((0,), (0,)))
    out_mine, out_gives = scatter_near(add(out_part[:, :64], *out_got).astype(BF16), zlo)
    out_got = scatter_send(*out_gives)
    gate_got, up_got = swap_core(gate_other), swap_core(up_other)
    grad_down = own_plus(hidden_all, cot_rows[:, :512], down_got)
    in_got, gate_got, up_got, grad_down, out_got = together(
        x_send(*in_relays), gate_got, up_got, grad_down, out_got
    )
    in_mine, in_gives = scatter_near(add(in_part[:, :64], *in_got).astype(BF16), zlo)
    in_got, grad_gate, grad_up, outputs = together(
        scatter_send(*in_gives),
        own_plus(x_rows[:, :512], act_gate, gate_got),
        own_plus(x_rows[:, :512], act_up, up_got),
        scattered(out_mine, out_got, zlo, core),
    )
    grad_inputs = scattered(in_mine, in_got, zlo, core)
    return outputs, grad_inputs, grad_gate, grad_up, grad_down


def solution(mesh):
    tokens = P(("depth", "inw"), "outw")
    w_in = P(("outw", "depth"), "inw")
    w_out = P("inw", ("outw", "depth"))
    return jax.shard_map(
        body,
        mesh=mesh,
        in_specs=(tokens, w_in, w_in, w_out, tokens),
        out_specs=(tokens, tokens, w_in, w_in, w_out),
        check_vma=False,
    )
```

profile of v0, /device:TPU:0, one launch (start us, length us, event | category | flops | bytes accessed | tf_op | source)
XLA Modules:
  0.0 222.2 jit_solution(8825006011286869010)
XLA Ops:
  2.3 2.1 collective-permute-start.2
  4.4 3.6 %collective-permute-start.3 = (bf16[3,16,1024]{2,1,0:T(8,128)(2,1)S(1)}, bf16[3,16,1024]{2,1,0:T(8,128)(2,1)S(1)}, u32[]{:S(2)}, u32[]{:S(2)}) collective-permute-start(bf16[3,16,1024]{2,1,0:T(8,128)(2,1)S(1)} %get-tuple-element.124), channel_id=1, source_target_pairs={{0,16},{4,20},{8,24},{12,28},{16,0},{20,4},{24,8},{28,12},{1,17},{... | collective-permute-start | bytes 294920 | tf_op jit(solution)/shard_map/ppermute | solution.py:16
  8.0 5.0 %collective-permute-done.3 = bf16[3,16,1024]{2,1,0:T(8,128)(2,1)S(1)} collective-permute-done((bf16[3,16,1024]{2,1,0:T(8,128)(2,1)S(1)}, bf16[3,16,1024]{2,1,0:T(8,128)(2,1)S(1)}, u32[]{:S(2)}, u32[]{:S(2)}) %collective-permute-start.3) | collective-permute-done | bytes 98336 | tf_op jit(solution)/shard_map/ppermute | solution.py:16
  12.9 1.9 collective-permute-done.4
  14.9 1.6 collective-permute-start.5
  16.5 2.1 collective-permute-start.6
  19.2 1.8 pad_maximum_fusion
  21.0 2.4 %collective-permute-done.7 = bf16[3,16,1024]{2,1,0:T(8,128)(2,1)S(1)} collective-permute-done((bf16[3,16,1024]{2,1,0:T(8,128)(2,1)S(1)}, bf16[3,16,1024]{2,1,0:T(8,128)(2,1)S(1)}, u32[]{:S(2)}, u32[]{:S(2)}) %collective-permute-start.7) | collective-permute-done | bytes 98336 | tf_op jit(solution)/shard_map/ppermute | solution.py:16
  23.4 1.3 collective-permute-start.8
  24.7 1.7 pad_maximum_fusion.1
  26.4 3.0 %collective-permute-done.8 = bf16[3,16,1024]{2,1,0:T(8,128)(2,1)S(1)} collective-permute-done((bf16[3,16,1024]{2,1,0:T(8,128)(2,1)S(1)}, bf16[3,16,1024]{2,1,0:T(8,128)(2,1)S(1)}, u32[]{:S(2)}, u32[]{:S(2)}) %collective-permute-start.8) | collective-permute-done | bytes 98336 | tf_op jit(solution)/shard_map/ppermute | solution.py:16
  31.1 4.2 %collective-permute-done.10 = bf16[3,32,1024]{2,1,0:T(8,128)(2,1)S(1)} collective-permute-done((bf16[3,32,1024]{2,1,0:T(8,128)(2,1)S(1)}, bf16[3,32,1024]{2,1,0:T(8,128)(2,1)S(1)}, u32[]{:S(2)}, u32[]{:S(2)}) %collective-permute-start.10) | collective-permute-done | bytes 196640 | tf_op jit(solution)/shard_map/ppermute | solution.py:16
  35.3 1.9 collective-permute-done.11
  45.5 1.6 collective-permute-start.18
  47.3 2.3 %collective-permute-start.26 = (bf16[2,128,1792]{2,1,0:T(8,128)(2,1)S(1)}, bf16[2,128,1792]{2,1,0:T(8,128)(2,1)S(1)}, u32[]{:S(2)}, u32[]{:S(2)}) collective-permute-start(bf16[2,128,1792]{2,1,0:T(8,128)(2,1)S(1)} %pad_maximum_fusion.16), channel_id=1, source_target_pairs={{0,3},{1,2},{2,1},{3,0},{4,7},{5,6},{6,5},{7,4},{8,11},{9,10},{10,... | collective-permute-start | bytes 2752520 | tf_op jit(solution)/shard_map/ppermute | solution.py:16
  49.8 8.9 %collective-permute-start.34 = (bf16[2,128,1792]{2,1,0:T(8,128)(2,1)S(1)}, bf16[2,128,1792]{2,1,0:T(8,128)(2,1)S(1)}, u32[]{:S(2)}, u32[]{:S(2)}) collective-permute-start(bf16[2,128,1792]{2,1,0:T(8,128)(2,1)S(1)} %pad_maximum_fusion.17), channel_id=1, source_target_pairs={{0,64},{32,96},{64,0},{96,32},{1,65},{33,97},{65,1},{97,33},{2,66}... | collective-permute-start | bytes 2752520 | tf_op jit(solution)/shard_map/ppermute | solution.py:16
  60.3 2.6 %collective-permute-start.16 = (bf16[3,32,1024]{2,1,0:T(8,128)(2,1)S(1)}, bf16[3,32,1024]{2,1,0:T(8,128)(2,1)S(1)}, u32[]{:S(2)}, u32[]{:S(2)}) collective-permute-start(bf16[3,32,1024]{2,1,0:T(8,128)(2,1)S(1)} %slice.201), channel_id=1, source_target_pairs={{0,12},{4,8},{8,4},{12,0},{16,28},{20,24},{24,20},{28,16},{1,13},{... | collective-permute-start | bytes 589832 | tf_op jit(solution)/shard_map/ppermute | solution.py:16
  62.9 2.2 collective-permute-done.15
  65.2 2.0 collective-permute-done.16
  67.2 1.2 convolution_convert_fusion.11
  68.4 1.2 convolution_convert_fusion.8
  71.1 1.2 convolution_convert_fusion.5
  72.3 2.1 collective-permute-start.33
  74.8 2.7 %collective-permute-start.19 = (bf16[2,64,1792]{2,1,0:T(8,128)(2,1)S(1)}, bf16[2,64,1792]{2,1,0:T(8,128)(2,1)S(1)}, u32[]{:S(2)}, u32[]{:S(2)}) collective-permute-start(bf16[2,64,1792]{2,1,0:T(8,128)(2,1)S(1)} %pad_maximum_fusion.22), channel_id=1, source_target_pairs={{0,3},{1,2},{2,1},{3,0},{4,7},{5,6},{6,5},{7,4},{8,11},{9,10},{10,... | collective-permute-start | bytes 1376264 | tf_op jit(solution)/shard_map/ppermute | solution.py:16
  77.8 4.2 %collective-permute-done.34 = bf16[2,128,1792]{2,1,0:T(8,128)(2,1)S(1)} collective-permute-done((bf16[2,128,1792]{2,1,0:T(8,128)(2,1)S(1)}, bf16[2,128,1792]{2,1,0:T(8,128)(2,1)S(1)}, u32[]{:S(2)}, u32[]{:S(2)}) %collective-permute-start.34) | collective-permute-done | bytes 917536 | tf_op jit(solution)/shard_map/ppermute | solution.py:16
  83.3 1.8 collective-permute-done.25
  85.8 6.0 %collective-permute-done.33 = bf16[1,128,1792]{2,1,0:T(8,128)(2,1)S(1)} collective-permute-done((bf16[1,128,1792]{2,1,0:T(8,128)(2,1)S(1)}, bf16[1,128,1792]{2,1,0:T(8,128)(2,1)S(1)}, u32[]{:S(2)}, u32[]{:S(2)}) %collective-permute-start.33) | collective-permute-done | bytes 458784 | tf_op jit(solution)/shard_map/ppermute | solution.py:16
  93.3 1.8 collective-permute-start.22
  95.1 6.5 %collective-permute-done.27 = bf16[2,64,1792]{2,1,0:T(8,128)(2,1)S(1)} collective-permute-done((bf16[2,64,1792]{2,1,0:T(8,128)(2,1)S(1)}, bf16[2,64,1792]{2,1,0:T(8,128)(2,1)S(1)}, u32[]{:S(2)}, u32[]{:S(2)}) %collective-permute-start.27) | collective-permute-done | bytes 458784 | tf_op jit(solution)/shard_map/ppermute | solution.py:16
  101.8 3.3 %collective-permute-done.29 = bf16[1,64,1792]{2,1,0:T(8,128)(2,1)S(1)} collective-permute-done((bf16[1,64,1792]{2,1,0:T(8,128)(2,1)S(1)}, bf16[1,64,1792]{2,1,0:T(8,128)(2,1)S(1)}, u32[]{:S(2)}, u32[]{:S(2)}) %collective-permute-start.29) | collective-permute-done | bytes 229408 | tf_op jit(solution)/shard_map/ppermute | solution.py:16
  105.2 1.3 collective-permute-start.30
  107.5 2.5 %collective-permute-start.38 = (bf16[64,1792]{1,0:T(8,128)(2,1)S(1)}, bf16[64,1792]{1,0:T(8,128)(2,1)S(1)}, u32[]{:S(2)}, u32[]{:S(2)}) collective-permute-start(bf16[64,1792]{1,0:T(8,128)(2,1)S(1)} %fusion.43), channel_id=1, source_target_pairs={{0,3},{1,2},{2,1},{3,0},{4,7},{5,6},{6,5},{7,4},{8,11},{9,10},{10,... | collective-permute-start | bytes 688136 | tf_op jit(solution)/shard_map/ppermute | solution.py:16
  111.9 9.2 %collective-permute-done.38 = bf16[64,1792]{1,0:T(8,128)(2,1)S(1)} collective-permute-done((bf16[64,1792]{1,0:T(8,128)(2,1)S(1)}, bf16[64,1792]{1,0:T(8,128)(2,1)S(1)}, u32[]{:S(2)}, u32[]{:S(2)}) %collective-permute-start.38) | collective-permute-done | bytes 229408 | tf_op jit(solution)/shard_map/ppermute | solution.py:16
  125.0 2.1 collective-permute-start.39
  128.2 2.8 %collective-permute-done.45 = bf16[1,64,1792]{2,1,0:T(8,128)(2,1)S(1)} collective-permute-done((bf16[1,64,1792]{2,1,0:T(8,128)(2,1)S(1)}, bf16[1,64,1792]{2,1,0:T(8,128)(2,1)S(1)}, u32[]{:S(2)}, u32[]{:S(2)}) %collective-permute-start.45) | collective-permute-done | bytes 229408 | tf_op jit(solution)/shard_map/ppermute | solution.py:16
  131.0 3.8 %collective-permute-start.41 = (bf16[1,64,1792]{2,1,0:T(8,128)(2,1)S(1)}, bf16[1,64,1792]{2,1,0:T(8,128)(2,1)S(1)}, u32[]{:S(2)}, u32[]{:S(2)}) collective-permute-start(bf16[1,64,1792]{2,1,0:T(8,128)(2,1)S(1)} %multiply_convert_fusion.2), channel_id=1, source_target_pairs={{0,3},{1,2},{2,1},{3,0},{4,7},{5,6},{6,5},{7,4},{8,11},{9,10},{10,... | collective-permute-start | bytes 688136 | tf_op jit(solution)/shard_map/ppermute | solution.py:16
  135.0 4.7 %collective-permute-done.43 = bf16[1,64,1792]{2,1,0:T(8,128)(2,1)S(1)} collective-permute-done((bf16[1,64,1792]{2,1,0:T(8,128)(2,1)S(1)}, bf16[1,64,1792]{2,1,0:T(8,128)(2,1)S(1)}, u32[]{:S(2)}, u32[]{:S(2)}) %collective-permute-start.43) | collective-permute-done | bytes 229408 | tf_op jit(solution)/shard_map/ppermute | solution.py:16
  141.3 3.2 %collective-permute-start.44 = (bf16[1,128,1792]{2,1,0:T(8,128)(2,1)S(1)}, bf16[1,128,1792]{2,1,0:T(8,128)(2,1)S(1)}, u32[]{:S(2)}, u32[]{:S(2)}) collective-permute-start(bf16[1,128,1792]{2,1,0:T(8,128)(2,1)S(1)} %maximum_select_fusion.12), channel_id=1, source_target_pairs={{0,3},{1,2},{2,1},{3,0},{4,7},{5,6},{6,5},{7,4},{8,11},{9,10},{10,... | collective-permute-start | bytes 1376264 | tf_op jit(solution)/shard_map/ppermute | solution.py:16
  145.0 2.1 collective-permute-start.24
  147.6 5.5 %collective-permute-done.46 = bf16[1,128,1792]{2,1,0:T(8,128)(2,1)S(1)} collective-permute-done((bf16[1,128,1792]{2,1,0:T(8,128)(2,1)S(1)}, bf16[1,128,1792]{2,1,0:T(8,128)(2,1)S(1)}, u32[]{:S(2)}, u32[]{:S(2)}) %collective-permute-start.46) | collective-permute-done | bytes 458784 | tf_op jit(solution)/shard_map/ppermute | solution.py:16
  154.2 1.1 fusion.5
  156.9 1.1 fusion.3
  159.1 3.8 %collective-permute-start.48 = (bf16[3,32,1024]{2,1,0:T(8,128)(2,1)S(1)}, bf16[3,32,1024]{2,1,0:T(8,128)(2,1)S(1)}, u32[]{:S(2)}, u32[]{:S(2)}) collective-permute-start(bf16[3,32,1024]{2,1,0:T(8,128)(2,1)S(1)} %get-tuple-element.263), channel_id=1, source_target_pairs={{0,12},{4,8},{8,4},{12,0},{16,28},{20,24},{24,20},{28,16},{1,13},{... | collective-permute-start | bytes 589832 | tf_op jit(solution)/shard_map/ppermute | solution.py:16
  162.9 1.6 convolution_convert_fusion.2
  164.5 2.0 collective-permute-done.48
  168.6 1.9 copy-done.3
  170.5 1.1 fusion.6
  173.5 1.1 fusion.7
  178.5 3.7 %collective-permute-start.50 = (bf16[3,32,1024]{2,1,0:T(8,128)(2,1)S(1)}, bf16[3,32,1024]{2,1,0:T(8,128)(2,1)S(1)}, u32[]{:S(2)}, u32[]{:S(2)}) collective-permute-start(bf16[3,32,1024]{2,1,0:T(8,128)(2,1)S(1)} %get-tuple-element.261), channel_id=1, source_target_pairs={{0,12},{4,8},{8,4},{12,0},{16,28},{20,24},{24,20},{28,16},{1,13},{... | collective-permute-start | bytes 589832 | tf_op jit(solution)/shard_map/ppermute | solution.py:16
  183.7 1.3 copy-done.13
  185.0 1.6 convolution_convert_fusion.1
  186.6 1.6 convolution_convert_fusion
  188.9 1.5 collective-permute-done.51
  190.3 1.4 collective-permute-done.52
  192.2 1.6 collective-permute-start.58
  195.0 2.8 %collective-permute-done.58 = bf16[3,16,1024]{2,1,0:T(8,128)(2,1)S(1)} collective-permute-done((bf16[3,16,1024]{2,1,0:T(8,128)(2,1)S(1)}, bf16[3,16,1024]{2,1,0:T(8,128)(2,1)S(1)}, u32[]{:S(2)}, u32[]{:S(2)}) %collective-permute-start.58) | collective-permute-done | bytes 98336 | tf_op jit(solution)/shard_map/ppermute | solution.py:16
  197.8 1.6 collective-permute-start.55
  200.2 2.1 collective-permute-start.60
  202.2 2.9 %add_convert_fusion.2 = bf16[1792,512]{1,0:T(8,128)(2,1)} fusion(bf16[1792,512]{1,0:T(8,128)(2,1)S(1)} %collective-permute-done.53, bf16[256,1792]{1,0:T(8,128)(2,1)S(1)} %maximum_select_fusion.8, bf16[256,1792]{1,0:T(8,128)(2,1)S(1)} %maximum_select_fusion.7, bf16[256,1792]{1,0:T(8,128)(2,1)S(1)} %maximum_select_fusion.6, bf16[768,1024]{1,0:T(8,128)(2,1)S(1)} %bitcast.339), kind=kOutput, calls=%fused_computation.5 | convolution fusion | flops 1420296192 | bytes 7208960 | tf_op jit(solution)/shard_map/dot_general | solution.py:231
  206.0 3.4 %collective-permute-done.55 = bf16[3,64,1024]{2,1,0:T(8,128)(2,1)S(1)} collective-permute-done((bf16[3,64,1024]{2,1,0:T(8,128)(2,1)S(1)}, bf16[3,64,1024]{2,1,0:T(8,128)(2,1)S(1)}, u32[]{:S(2)}, u32[]{:S(2)}) %collective-permute-start.55) | collective-permute-done | bytes 393248 | tf_op jit(solution)/shard_map/ppermute | solution.py:16
  209.7 1.6 collective-permute-start.61
  212.2 2.3 %collective-permute-start.63 = (bf16[3,16,1024]{2,1,0:T(8,128)(2,1)S(1)}, bf16[3,16,1024]{2,1,0:T(8,128)(2,1)S(1)}, u32[]{:S(2)}, u32[]{:S(2)}) collective-permute-start(bf16[3,16,1024]{2,1,0:T(8,128)(2,1)S(1)} %get-tuple-element.227), channel_id=1, source_target_pairs={{0,80},{4,84},{8,88},{12,92},{16,64},{20,68},{24,72},{28,76},{32,1... | collective-permute-start | bytes 294920 | tf_op jit(solution)/shard_map/ppermute | solution.py:32
  214.5 2.9 %add_convert_fusion.1 = bf16[512,1792]{1,0:T(8,128)(2,1)} fusion(bf16[512,1792]{1,0:T(8,128)(2,1)S(1)} %collective-permute-done.56, bf16[256,1792]{1,0:T(8,128)(2,1)S(1)} %get-tuple-element.252, bf16[256,1792]{1,0:T(8,128)(2,1)S(1)} %get-tuple-element.250, bf16[256,1792]{1,0:T(8,128)(2,1)S(1)} %get-tuple-element.248, bf16[768,1024]{1,0:T(8,128)(2,1)S(1)} %bitcast.342), kind=kOutput, calls=%fused_computation.4 | convolution fusion | flops 1420296192 | bytes 7208960 | tf_op jit(solution)/shard_map/dot_general | solution.py:231
  217.4 2.9 %add_convert_fusion = bf16[512,1792]{1,0:T(8,128)(2,1)} fusion(bf16[512,1792]{1,0:T(8,128)(2,1)S(1)} %collective-permute-done.57, bf16[256,1792]{1,0:T(8,128)(2,1)S(1)} %get-tuple-element.251, bf16[256,1792]{1,0:T(8,128)(2,1)S(1)} %get-tuple-element.249, bf16[256,1792]{1,0:T(8,128)(2,1)S(1)} %get-tuple-element.247, bf16[768,1024]{1,0:T(8,128)(2,1)S(1)} %bitcast.343), kind=kOutput, calls=%fused_computation.3 | convolution fusion | flops 1420296192 | bytes 7208960 | tf_op jit(solution)/shard_map/dot_general | solution.py:231
  (244 shorter events, 49.9 us)
Async XLA Ops:
  0.6 14.1 %collective-permute-start = (bf16[512,1792]{1,0:T(8,128)(2,1)}, bf16[512,1792]{1,0:T(8,128)(2,1)}, u32[]{:S(2)}, u32[]{:S(2)}) collective-permute-start(bf16[512,1792]{1,0:T(8,128)(2,1)} %param.6), channel_id=1, source_target_pairs={{0,32},{32,0},{64,96},{96,64},{1,33},{33,1},{65,97},{97,65},{2,34}... | collective-permute-start | bytes 5505032 | tf_op jit(solution)/shard_map/ppermute | solution.py:16
  0.7 14.1 %collective-permute-start.1 = (bf16[512,1792]{1,0:T(8,128)(2,1)}, bf16[512,1792]{1,0:T(8,128)(2,1)}, u32[]{:S(2)}, u32[]{:S(2)}) collective-permute-start(bf16[512,1792]{1,0:T(8,128)(2,1)} %param.7), channel_id=1, source_target_pairs={{0,32},{32,0},{64,96},{96,64},{1,33},{33,1},{65,97},{97,65},{2,34}... | collective-permute-start | bytes 5505032 | tf_op jit(solution)/shard_map/ppermute | solution.py:16
  2.3 5.7 %collective-permute-start.2 = (bf16[3,16,1024]{2,1,0:T(8,128)(2,1)S(1)}, bf16[3,16,1024]{2,1,0:T(8,128)(2,1)S(1)}, u32[]{:S(2)}, u32[]{:S(2)}) collective-permute-start(bf16[3,16,1024]{2,1,0:T(8,128)(2,1)S(1)} %get-tuple-element.125), channel_id=1, source_target_pairs={{0,64},{32,96},{64,0},{96,32},{1,65},{33,97},{65,1},{97,33},{2,66}... | collective-permute-start | bytes 294920 | tf_op jit(solution)/shard_map/ppermute | solution.py:16
  4.4 8.6 %collective-permute-start.3 = (bf16[3,16,1024]{2,1,0:T(8,128)(2,1)S(1)}, bf16[3,16,1024]{2,1,0:T(8,128)(2,1)S(1)}, u32[]{:S(2)}, u32[]{:S(2)}) collective-permute-start(bf16[3,16,1024]{2,1,0:T(8,128)(2,1)S(1)} %get-tuple-element.124), channel_id=1, source_target_pairs={{0,16},{4,20},{8,24},{12,28},{16,0},{20,4},{24,8},{28,12},{1,17},{... | collective-permute-start | bytes 294920 | tf_op jit(solution)/shard_map/ppermute | solution.py:16
  7.9 6.8 %collective-permute-start.4 = (bf16[3,16,1024]{2,1,0:T(8,128)(2,1)S(1)}, bf16[3,16,1024]{2,1,0:T(8,128)(2,1)S(1)}, u32[]{:S(2)}, u32[]{:S(2)}) collective-permute-start(bf16[3,16,1024]{2,1,0:T(8,128)(2,1)S(1)} %get-tuple-element.125), channel_id=1, source_target_pairs={{0,80},{4,84},{8,88},{12,92},{16,64},{20,68},{24,72},{28,76},{32,1... | collective-permute-start | bytes 294920 | tf_op jit(solution)/shard_map/ppermute | solution.py:32
  7.9 29.2 %collective-permute-start.12 = (bf16[1792,512]{1,0:T(8,128)(2,1)}, bf16[1792,512]{1,0:T(8,128)(2,1)S(1)}, u32[]{:S(2)}, u32[]{:S(2)}) collective-permute-start(bf16[1792,512]{1,0:T(8,128)(2,1)} %param.8), channel_id=1, source_target_pairs={{0,32},{32,0},{64,96},{96,64},{1,33},{33,1},{65,97},{97,65},{2,34}... | collective-permute-start | bytes 5505032 | tf_op jit(solution)/shard_map/ppermute | solution.py:16
  14.9 14.6 %collective-permute-start.5 = (bf16[3,64,1024]{2,1,0:T(8,128)(2,1)S(1)}, bf16[3,64,1024]{2,1,0:T(8,128)(2,1)S(1)}, u32[]{:S(2)}, u32[]{:S(2)}) collective-permute-start(bf16[3,64,1024]{2,1,0:T(8,128)(2,1)S(1)} %pad_maximum_fusion.33), channel_id=1, source_target_pairs={{0,4},{4,0},{8,12},{12,8},{16,20},{20,16},{24,28},{28,24},{1,5},{5... | collective-permute-start | bytes 1179656 | tf_op jit(solution)/shard_map/ppermute | solution.py:16
  16.5 13.0 %collective-permute-start.6 = (bf16[3,64,1024]{2,1,0:T(8,128)(2,1)S(1)}, bf16[3,64,1024]{2,1,0:T(8,128)(2,1)S(1)}, u32[]{:S(2)}, u32[]{:S(2)}) collective-permute-start(bf16[3,64,1024]{2,1,0:T(8,128)(2,1)S(1)} %pad_maximum_fusion.33), channel_id=1, source_target_pairs={{0,12},{4,8},{8,4},{12,0},{16,28},{20,24},{24,20},{28,16},{1,13},{... | collective-permute-start | bytes 1179656 | tf_op jit(solution)/shard_map/ppermute | solution.py:16
  18.7 4.7 %collective-permute-start.7 = (bf16[3,16,1024]{2,1,0:T(8,128)(2,1)S(1)}, bf16[3,16,1024]{2,1,0:T(8,128)(2,1)S(1)}, u32[]{:S(2)}, u32[]{:S(2)}) collective-permute-start(bf16[3,16,1024]{2,1,0:T(8,128)(2,1)S(1)} %pad_maximum_fusion.42), channel_id=1, source_target_pairs={{0,64},{32,96},{64,0},{96,32},{1,65},{33,97},{65,1},{97,33},{2,66}... | collective-permute-start | bytes 294920 | tf_op jit(solution)/shard_map/ppermute | solution.py:16
  18.8 10.7 %collective-permute-start.9 = (bf16[3,16,1024]{2,1,0:T(8,128)(2,1)S(1)}, bf16[3,16,1024]{2,1,0:T(8,128)(2,1)S(1)}, u32[]{:S(2)}, u32[]{:S(2)}) collective-permute-start(bf16[3,16,1024]{2,1,0:T(8,128)(2,1)S(1)} %pad_maximum_fusion.42), channel_id=1, source_target_pairs={{0,80},{4,84},{8,88},{12,92},{16,64},{20,68},{24,72},{28,76},{32,1... | collective-permute-start | bytes 294920 | tf_op jit(solution)/shard_map/ppermute | solution.py:32
  23.4 6.1 %collective-permute-start.8 = (bf16[3,16,1024]{2,1,0:T(8,128)(2,1)S(1)}, bf16[3,16,1024]{2,1,0:T(8,128)(2,1)S(1)}, u32[]{:S(2)}, u32[]{:S(2)}) collective-permute-start(bf16[3,16,1024]{2,1,0:T(8,128)(2,1)S(1)} %pad_maximum_fusion.41), channel_id=1, source_target_pairs={{0,16},{4,20},{8,24},{12,28},{16,0},{20,4},{24,8},{28,12},{1,17},{... | collective-permute-start | bytes 294920 | tf_op jit(solution)/shard_map/ppermute | solution.py:16
  29.5 5.7 %collective-permute-start.10 = (bf16[3,32,1024]{2,1,0:T(8,128)(2,1)S(1)}, bf16[3,32,1024]{2,1,0:T(8,128)(2,1)S(1)}, u32[]{:S(2)}, u32[]{:S(2)}) collective-permute-start(bf16[3,32,1024]{2,1,0:T(8,128)(2,1)S(1)} %slice.198), channel_id=1, source_target_pairs={{0,4},{4,0},{8,12},{12,8},{16,20},{20,16},{24,28},{28,24},{1,5},{5... | collective-permute-start | bytes 589832 | tf_op jit(solution)/shard_map/ppermute | solution.py:16
  30.2 7.0 %collective-permute-start.11 = (bf16[3,32,1024]{2,1,0:T(8,128)(2,1)S(1)}, bf16[3,32,1024]{2,1,0:T(8,128)(2,1)S(1)}, u32[]{:S(2)}, u32[]{:S(2)}) collective-permute-start(bf16[3,32,1024]{2,1,0:T(8,128)(2,1)S(1)} %slice.199), channel_id=1, source_target_pairs={{0,12},{4,8},{8,4},{12,0},{16,28},{20,24},{24,20},{28,16},{1,13},{... | collective-permute-start | bytes 589832 | tf_op jit(solution)/shard_map/ppermute | solution.py:16
  37.2 22.2 %collective-permute-start.13 = (bf16[3,64,1024]{2,1,0:T(8,128)(2,1)S(1)}, bf16[3,64,1024]{2,1,0:T(8,128)(2,1)S(1)}, u32[]{:S(2)}, u32[]{:S(2)}) collective-permute-start(bf16[3,64,1024]{2,1,0:T(8,128)(2,1)S(1)} %pad_maximum_fusion.34), channel_id=1, source_target_pairs={{0,4},{4,0},{8,12},{12,8},{16,20},{20,16},{24,28},{28,24},{1,5},{5... | collective-permute-start | bytes 1179656 | tf_op jit(solution)/shard_map/ppermute | solution.py:16
  37.3 22.0 %collective-permute-start.14 = (bf16[3,64,1024]{2,1,0:T(8,128)(2,1)S(1)}, bf16[3,64,1024]{2,1,0:T(8,128)(2,1)S(1)}, u32[]{:S(2)}, u32[]{:S(2)}) collective-permute-start(bf16[3,64,1024]{2,1,0:T(8,128)(2,1)S(1)} %pad_maximum_fusion.34), channel_id=1, source_target_pairs={{0,12},{4,8},{8,4},{12,0},{16,28},{20,24},{24,20},{28,16},{1,13},{... | collective-permute-start | bytes 1179656 | tf_op jit(solution)/shard_map/ppermute | solution.py:16
  45.5 26.8 %collective-permute-start.18 = (bf16[2,128,1792]{2,1,0:T(8,128)(2,1)S(1)}, bf16[2,128,1792]{2,1,0:T(8,128)(2,1)S(1)}, u32[]{:S(2)}, u32[]{:S(2)}) collective-permute-start(bf16[2,128,1792]{2,1,0:T(8,128)(2,1)S(1)} %pad_maximum_fusion.15), channel_id=1, source_target_pairs={{0,1},{1,0},{2,3},{3,2},{4,5},{5,4},{6,7},{7,6},{8,9},{9,8},{10,11... | collective-permute-start | bytes 2752520 | tf_op jit(solution)/shard_map/ppermute | solution.py:16
  47.3 27.4 %collective-permute-start.26 = (bf16[2,128,1792]{2,1,0:T(8,128)(2,1)S(1)}, bf16[2,128,1792]{2,1,0:T(8,128)(2,1)S(1)}, u32[]{:S(2)}, u32[]{:S(2)}) collective-permute-start(bf16[2,128,1792]{2,1,0:T(8,128)(2,1)S(1)} %pad_maximum_fusion.16), channel_id=1, source_target_pairs={{0,3},{1,2},{2,1},{3,0},{4,7},{5,6},{6,5},{7,4},{8,11},{9,10},{10,... | collective-permute-start | bytes 2752520 | tf_op jit(solution)/shard_map/ppermute | solution.py:16
  49.8 32.2 %collective-permute-start.34 = (bf16[2,128,1792]{2,1,0:T(8,128)(2,1)S(1)}, bf16[2,128,1792]{2,1,0:T(8,128)(2,1)S(1)}, u32[]{:S(2)}, u32[]{:S(2)}) collective-permute-start(bf16[2,128,1792]{2,1,0:T(8,128)(2,1)S(1)} %pad_maximum_fusion.17), channel_id=1, source_target_pairs={{0,64},{32,96},{64,0},{96,32},{1,65},{33,97},{65,1},{97,33},{2,66}... | collective-permute-start | bytes 2752520 | tf_op jit(solution)/shard_map/ppermute | solution.py:16
  59.4 5.7 %collective-permute-start.15 = (bf16[3,32,1024]{2,1,0:T(8,128)(2,1)S(1)}, bf16[3,32,1024]{2,1,0:T(8,128)(2,1)S(1)}, u32[]{:S(2)}, u32[]{:S(2)}) collective-permute-start(bf16[3,32,1024]{2,1,0:T(8,128)(2,1)S(1)} %slice.200), channel_id=1, source_target_pairs={{0,4},{4,0},{8,12},{12,8},{16,20},{20,16},{24,28},{28,24},{1,5},{5... | collective-permute-start | bytes 589832 | tf_op jit(solution)/shard_map/ppermute | solution.py:16
  60.3 6.9 %collective-permute-start.16 = (bf16[3,32,1024]{2,1,0:T(8,128)(2,1)S(1)}, bf16[3,32,1024]{2,1,0:T(8,128)(2,1)S(1)}, u32[]{:S(2)}, u32[]{:S(2)}) collective-permute-start(bf16[3,32,1024]{2,1,0:T(8,128)(2,1)S(1)} %slice.201), channel_id=1, source_target_pairs={{0,12},{4,8},{8,4},{12,0},{16,28},{20,24},{24,20},{28,16},{1,13},{... | collective-permute-start | bytes 589832 | tf_op jit(solution)/shard_map/ppermute | solution.py:16
  69.6 12.8 %collective-permute-start.17 = (bf16[1,128,1792]{2,1,0:T(8,128)(2,1)S(1)}, bf16[1,128,1792]{2,1,0:T(8,128)(2,1)S(1)}, u32[]{:S(2)}, u32[]{:S(2)}) collective-permute-start(bf16[1,128,1792]{2,1,0:T(8,128)(2,1)S(1)} %dynamic-slice_bitcast_fusion.8), channel_id=1, source_target_pairs={{0,1},{1,0},{2,3},{3,2},{4,5},{5,4},{6,7},{7,6},{8,9},{9,8},{10,11... | collective-permute-start | bytes 1376264 | tf_op jit(solution)/shard_map/ppermute | solution.py:16
  70.4 14.7 %collective-permute-start.25 = (bf16[1,128,1792]{2,1,0:T(8,128)(2,1)S(1)}, bf16[1,128,1792]{2,1,0:T(8,128)(2,1)S(1)}, u32[]{:S(2)}, u32[]{:S(2)}) collective-permute-start(bf16[1,128,1792]{2,1,0:T(8,128)(2,1)S(1)} %dynamic-slice_bitcast_fusion.5), channel_id=1, source_target_pairs={{0,3},{1,2},{2,1},{3,0},{4,7},{5,6},{6,5},{7,4},{8,11},{9,10},{10,... | collective-permute-start | bytes 1376264 | tf_op jit(solution)/shard_map/ppermute | solution.py:16
  72.3 19.5 %collective-permute-start.33 = (bf16[1,128,1792]{2,1,0:T(8,128)(2,1)S(1)}, bf16[1,128,1792]{2,1,0:T(8,128)(2,1)S(1)}, u32[]{:S(2)}, u32[]{:S(2)}) collective-permute-start(bf16[1,128,1792]{2,1,0:T(8,128)(2,1)S(1)} %dynamic-slice_bitcast_fusion.2), channel_id=1, source_target_pairs={{0,64},{32,96},{64,0},{96,32},{1,65},{33,97},{65,1},{97,33},{2,66}... | collective-permute-start | bytes 1376264 | tf_op jit(solution)/shard_map/ppermute | solution.py:16
  74.8 17.2 %collective-permute-start.19 = (bf16[2,64,1792]{2,1,0:T(8,128)(2,1)S(1)}, bf16[2,64,1792]{2,1,0:T(8,128)(2,1)S(1)}, u32[]{:S(2)}, u32[]{:S(2)}) collective-permute-start(bf16[2,64,1792]{2,1,0:T(8,128)(2,1)S(1)} %pad_maximum_fusion.22), channel_id=1, source_target_pairs={{0,3},{1,2},{2,1},{3,0},{4,7},{5,6},{6,5},{7,4},{8,11},{9,10},{10,... | collective-permute-start | bytes 1376264 | tf_op jit(solution)/shard_map/ppermute | solution.py:16
  82.0 19.7 %collective-permute-start.27 = (bf16[2,64,1792]{2,1,0:T(8,128)(2,1)S(1)}, bf16[2,64,1792]{2,1,0:T(8,128)(2,1)S(1)}, u32[]{:S(2)}, u32[]{:S(2)}) collective-permute-start(bf16[2,64,1792]{2,1,0:T(8,128)(2,1)S(1)} %pad_maximum_fusion.25), channel_id=1, source_target_pairs={{0,64},{32,96},{64,0},{96,32},{1,65},{33,97},{65,1},{97,33},{2,66}... | collective-permute-start | bytes 1376264 | tf_op jit(solution)/shard_map/ppermute | solution.py:16
  82.4 24.1 %collective-permute-start.35 = (bf16[2,64,1792]{2,1,0:T(8,128)(2,1)S(1)}, bf16[2,64,1792]{2,1,0:T(8,128)(2,1)S(1)}, u32[]{:S(2)}, u32[]{:S(2)}) collective-permute-start(bf16[2,64,1792]{2,1,0:T(8,128)(2,1)S(1)} %pad_maximum_fusion.28), channel_id=1, source_target_pairs={{0,1},{1,0},{2,3},{3,2},{4,5},{5,4},{6,7},{7,6},{8,9},{9,8},{10,11... | collective-permute-start | bytes 1376264 | tf_op jit(solution)/shard_map/ppermute | solution.py:16
  85.1 8.1 %collective-permute-start.21 = (bf16[1,64,1792]{2,1,0:T(8,128)(2,1)S(1)}, bf16[1,64,1792]{2,1,0:T(8,128)(2,1)S(1)}, u32[]{:S(2)}, u32[]{:S(2)}) collective-permute-start(bf16[1,64,1792]{2,1,0:T(8,128)(2,1)S(1)} %dynamic-slice_bitcast_fusion.15), channel_id=1, source_target_pairs={{0,3},{1,2},{2,1},{3,0},{4,7},{5,6},{6,5},{7,4},{8,11},{9,10},{10,... | collective-permute-start | bytes 688136 | tf_op jit(solution)/shard_map/ppermute | solution.py:16
  91.8 13.3 %collective-permute-start.29 = (bf16[1,64,1792]{2,1,0:T(8,128)(2,1)S(1)}, bf16[1,64,1792]{2,1,0:T(8,128)(2,1)S(1)}, u32[]{:S(2)}, u32[]{:S(2)}) collective-permute-start(bf16[1,64,1792]{2,1,0:T(8,128)(2,1)S(1)} %dynamic-slice_bitcast_fusion.12), channel_id=1, source_target_pairs={{0,64},{32,96},{64,0},{96,32},{1,65},{33,97},{65,1},{97,33},{2,66}... | collective-permute-start | bytes 688136 | tf_op jit(solution)/shard_map/ppermute | solution.py:16
  92.0 15.5 %collective-permute-start.37 = (bf16[1,64,1792]{2,1,0:T(8,128)(2,1)S(1)}, bf16[1,64,1792]{2,1,0:T(8,128)(2,1)S(1)}, u32[]{:S(2)}, u32[]{:S(2)}) collective-permute-start(bf16[1,64,1792]{2,1,0:T(8,128)(2,1)S(1)} %dynamic-slice_bitcast_fusion.9), channel_id=1, source_target_pairs={{0,1},{1,0},{2,3},{3,2},{4,5},{5,4},{6,7},{7,6},{8,9},{9,8},{10,11... | collective-permute-start | bytes 688136 | tf_op jit(solution)/shard_map/ppermute | solution.py:16
  93.3 16.8 %collective-permute-start.22 = (bf16[64,1792]{1,0:T(8,128)(2,1)S(1)}, bf16[64,1792]{1,0:T(8,128)(2,1)S(1)}, u32[]{:S(2)}, u32[]{:S(2)}) collective-permute-start(bf16[64,1792]{1,0:T(8,128)(2,1)S(1)} %fusion.49), channel_id=1, source_target_pairs={{0,64},{32,96},{64,0},{96,32},{1,65},{33,97},{65,1},{97,33},{2,66}... | collective-permute-start | bytes 688136 | tf_op jit(solution)/shard_map/ppermute | solution.py:16
  105.2 6.8 %collective-permute-start.30 = (bf16[64,1792]{1,0:T(8,128)(2,1)S(1)}, bf16[64,1792]{1,0:T(8,128)(2,1)S(1)}, u32[]{:S(2)}, u32[]{:S(2)}) collective-permute-start(bf16[64,1792]{1,0:T(8,128)(2,1)S(1)} %fusion.46), channel_id=1, source_target_pairs={{0,1},{1,0},{2,3},{3,2},{4,5},{5,4},{6,7},{7,6},{8,9},{9,8},{10,11... | collective-permute-start | bytes 688136 | tf_op jit(solution)/shard_map/ppermute | solution.py:16
  106.6 14.5 %collective-permute-start.36 = (bf16[2,64,1792]{2,1,0:T(8,128)(2,1)S(1)}, bf16[2,64,1792]{2,1,0:T(8,128)(2,1)S(1)}, u32[]{:S(2)}, u32[]{:S(2)}) collective-permute-start(bf16[2,64,1792]{2,1,0:T(8,128)(2,1)S(1)} %pad_maximum_fusion.29), channel_id=1, source_target_pairs={{0,3},{1,2},{2,1},{3,0},{4,7},{5,6},{6,5},{7,4},{8,11},{9,10},{10,... | collective-permute-start | bytes 1376264 | tf_op jit(solution)/shard_map/ppermute | solution.py:16
  107.5 13.6 %collective-permute-start.38 = (bf16[64,1792]{1,0:T(8,128)(2,1)S(1)}, bf16[64,1792]{1,0:T(8,128)(2,1)S(1)}, u32[]{:S(2)}, u32[]{:S(2)}) collective-permute-start(bf16[64,1792]{1,0:T(8,128)(2,1)S(1)} %fusion.43), channel_id=1, source_target_pairs={{0,3},{1,2},{2,1},{3,0},{4,7},{5,6},{6,5},{7,4},{8,11},{9,10},{10,... | collective-permute-start | bytes 688136 | tf_op jit(solution)/shard_map/ppermute | solution.py:16
  110.1 11.8 %collective-permute-start.20 = (bf16[2,64,1792]{2,1,0:T(8,128)(2,1)S(1)}, bf16[2,64,1792]{2,1,0:T(8,128)(2,1)S(1)}, u32[]{:S(2)}, u32[]{:S(2)}) collective-permute-start(bf16[2,64,1792]{2,1,0:T(8,128)(2,1)S(1)} %pad_maximum_fusion.23), channel_id=1, source_target_pairs={{0,64},{32,96},{64,0},{96,32},{1,65},{33,97},{65,1},{97,33},{2,66}... | collective-permute-start | bytes 1376264 | tf_op jit(solution)/shard_map/ppermute | solution.py:16
  110.1 11.4 %collective-permute-start.28 = (bf16[2,64,1792]{2,1,0:T(8,128)(2,1)S(1)}, bf16[2,64,1792]{2,1,0:T(8,128)(2,1)S(1)}, u32[]{:S(2)}, u32[]{:S(2)}) collective-permute-start(bf16[2,64,1792]{2,1,0:T(8,128)(2,1)S(1)} %pad_maximum_fusion.26), channel_id=1, source_target_pairs={{0,1},{1,0},{2,3},{3,2},{4,5},{5,4},{6,7},{7,6},{8,9},{9,8},{10,11... | collective-permute-start | bytes 1376264 | tf_op jit(solution)/shard_map/ppermute | solution.py:16
  122.6 22.1 %collective-permute-start.23 = (bf16[2,64,1792]{2,1,0:T(8,128)(2,1)S(1)}, bf16[2,64,1792]{2,1,0:T(8,128)(2,1)S(1)}, u32[]{:S(2)}, u32[]{:S(2)}) collective-permute-start(bf16[2,64,1792]{2,1,0:T(8,128)(2,1)S(1)} %pad_maximum_fusion.24), channel_id=1, source_target_pairs={{0,3},{1,2},{2,1},{3,0},{4,7},{5,6},{6,5},{7,4},{8,11},{9,10},{10,... | collective-permute-start | bytes 1376264 | tf_op jit(solution)/shard_map/ppermute | solution.py:16
  123.7 21.3 %collective-permute-start.31 = (bf16[2,64,1792]{2,1,0:T(8,128)(2,1)S(1)}, bf16[2,64,1792]{2,1,0:T(8,128)(2,1)S(1)}, u32[]{:S(2)}, u32[]{:S(2)}) collective-permute-start(bf16[2,64,1792]{2,1,0:T(8,128)(2,1)S(1)} %pad_maximum_fusion.27), channel_id=1, source_target_pairs={{0,64},{32,96},{64,0},{96,32},{1,65},{33,97},{65,1},{97,33},{2,66}... | collective-permute-start | bytes 1376264 | tf_op jit(solution)/shard_map/ppermute | solution.py:16
  124.7 6.3 %collective-permute-start.45 = (bf16[1,64,1792]{2,1,0:T(8,128)(2,1)S(1)}, bf16[1,64,1792]{2,1,0:T(8,128)(2,1)S(1)}, u32[]{:S(2)}, u32[]{:S(2)}) collective-permute-start(bf16[1,64,1792]{2,1,0:T(8,128)(2,1)S(1)} %multiply_convert_fusion), channel_id=1, source_target_pairs={{0,1},{1,0},{2,3},{3,2},{4,5},{5,4},{6,7},{7,6},{8,9},{9,8},{10,11... | collective-permute-start | bytes 688136 | tf_op jit(solution)/shard_map/ppermute | solution.py:16
  125.0 22.3 %collective-permute-start.39 = (bf16[2,64,1792]{2,1,0:T(8,128)(2,1)S(1)}, bf16[2,64,1792]{2,1,0:T(8,128)(2,1)S(1)}, u32[]{:S(2)}, u32[]{:S(2)}) collective-permute-start(bf16[2,64,1792]{2,1,0:T(8,128)(2,1)S(1)} %pad_maximum_fusion.30), channel_id=1, source_target_pairs={{0,1},{1,0},{2,3},{3,2},{4,5},{5,4},{6,7},{7,6},{8,9},{9,8},{10,11... | collective-permute-start | bytes 1376264 | tf_op jit(solution)/shard_map/ppermute | solution.py:16
  127.1 12.5 %collective-permute-start.43 = (bf16[1,64,1792]{2,1,0:T(8,128)(2,1)S(1)}, bf16[1,64,1792]{2,1,0:T(8,128)(2,1)S(1)}, u32[]{:S(2)}, u32[]{:S(2)}) collective-permute-start(bf16[1,64,1792]{2,1,0:T(8,128)(2,1)S(1)} %multiply_convert_fusion.1), channel_id=1, source_target_pairs={{0,64},{32,96},{64,0},{96,32},{1,65},{33,97},{65,1},{97,33},{2,66}... | collective-permute-start | bytes 688136 | tf_op jit(solution)/shard_map/ppermute | solution.py:16
  131.0 10.3 %collective-permute-start.41 = (bf16[1,64,1792]{2,1,0:T(8,128)(2,1)S(1)}, bf16[1,64,1792]{2,1,0:T(8,128)(2,1)S(1)}, u32[]{:S(2)}, u32[]{:S(2)}) collective-permute-start(bf16[1,64,1792]{2,1,0:T(8,128)(2,1)S(1)} %multiply_convert_fusion.2), channel_id=1, source_target_pairs={{0,3},{1,2},{2,1},{3,0},{4,7},{5,6},{6,5},{7,4},{8,11},{9,10},{10,... | collective-permute-start | bytes 688136 | tf_op jit(solution)/shard_map/ppermute | solution.py:16
  139.6 13.5 %collective-permute-start.46 = (bf16[1,128,1792]{2,1,0:T(8,128)(2,1)S(1)}, bf16[1,128,1792]{2,1,0:T(8,128)(2,1)S(1)}, u32[]{:S(2)}, u32[]{:S(2)}) collective-permute-start(bf16[1,128,1792]{2,1,0:T(8,128)(2,1)S(1)} %maximum_select_fusion.14), channel_id=1, source_target_pairs={{0,64},{32,96},{64,0},{96,32},{1,65},{33,97},{65,1},{97,33},{2,66}... | collective-permute-start | bytes 1376264 | tf_op jit(solution)/shard_map/ppermute | solution.py:16
  141.3 14.1 %collective-permute-start.44 = (bf16[1,128,1792]{2,1,0:T(8,128)(2,1)S(1)}, bf16[1,128,1792]{2,1,0:T(8,128)(2,1)S(1)}, u32[]{:S(2)}, u32[]{:S(2)}) collective-permute-start(bf16[1,128,1792]{2,1,0:T(8,128)(2,1)S(1)} %maximum_select_fusion.12), channel_id=1, source_target_pairs={{0,3},{1,2},{2,1},{3,0},{4,7},{5,6},{6,5},{7,4},{8,11},{9,10},{10,... | collective-permute-start | bytes 1376264 | tf_op jit(solution)/shard_map/ppermute | solution.py:16
  144.8 12.0 %collective-permute-start.42 = (bf16[1,128,1792]{2,1,0:T(8,128)(2,1)S(1)}, bf16[1,128,1792]{2,1,0:T(8,128)(2,1)S(1)}, u32[]{:S(2)}, u32[]{:S(2)}) collective-permute-start(bf16[1,128,1792]{2,1,0:T(8,128)(2,1)S(1)} %maximum_select_fusion.10), channel_id=1, source_target_pairs={{0,1},{1,0},{2,3},{3,2},{4,5},{5,4},{6,7},{7,6},{8,9},{9,8},{10,11... | collective-permute-start | bytes 1376264 | tf_op jit(solution)/shard_map/ppermute | solution.py:16
  145.0 21.5 %collective-permute-start.24 = (bf16[2,128,1792]{2,1,0:T(8,128)(2,1)S(1)}, bf16[2,128,1792]{2,1,0:T(8,128)(2,1)S(1)}, u32[]{:S(2)}, u32[]{:S(2)}) collective-permute-start(bf16[2,128,1792]{2,1,0:T(8,128)(2,1)S(1)} %maximum_select_fusion.3), channel_id=1, source_target_pairs={{0,1},{1,0},{2,3},{3,2},{4,5},{5,4},{6,7},{7,6},{8,9},{9,8},{10,11... | collective-permute-start | bytes 2752520 | tf_op jit(solution)/shard_map/ppermute | solution.py:16
  147.4 19.2 %collective-permute-start.32 = (bf16[2,128,1792]{2,1,0:T(8,128)(2,1)S(1)}, bf16[2,128,1792]{2,1,0:T(8,128)(2,1)S(1)}, u32[]{:S(2)}, u32[]{:S(2)}) collective-permute-start(bf16[2,128,1792]{2,1,0:T(8,128)(2,1)S(1)} %maximum_select_fusion.4), channel_id=1, source_target_pairs={{0,3},{1,2},{2,1},{3,0},{4,7},{5,6},{6,5},{7,4},{8,11},{9,10},{10,... | collective-permute-start | bytes 2752520 | tf_op jit(solution)/shard_map/ppermute | solution.py:16
  153.1 13.4 %collective-permute-start.40 = (bf16[2,128,1792]{2,1,0:T(8,128)(2,1)S(1)}, bf16[2,128,1792]{2,1,0:T(8,128)(2,1)S(1)}, u32[]{:S(2)}, u32[]{:S(2)}) collective-permute-start(bf16[2,128,1792]{2,1,0:T(8,128)(2,1)S(1)} %maximum_select_fusion.5), channel_id=1, source_target_pairs={{0,64},{32,96},{64,0},{96,32},{1,65},{33,97},{65,1},{97,33},{2,66}... | collective-permute-start | bytes 2752520 | tf_op jit(solution)/shard_map/ppermute | solution.py:16
  158.2 6.4 %collective-permute-start.47 = (bf16[3,32,1024]{2,1,0:T(8,128)(2,1)S(1)}, bf16[3,32,1024]{2,1,0:T(8,128)(2,1)S(1)}, u32[]{:S(2)}, u32[]{:S(2)}) collective-permute-start(bf16[3,32,1024]{2,1,0:T(8,128)(2,1)S(1)} %get-tuple-element.264), channel_id=1, source_target_pairs={{0,4},{4,0},{8,12},{12,8},{16,20},{20,16},{24,28},{28,24},{1,5},{5... | collective-permute-start | bytes 589832 | tf_op jit(solution)/shard_map/ppermute | solution.py:16
  159.1 7.4 %collective-permute-start.48 = (bf16[3,32,1024]{2,1,0:T(8,128)(2,1)S(1)}, bf16[3,32,1024]{2,1,0:T(8,128)(2,1)S(1)}, u32[]{:S(2)}, u32[]{:S(2)}) collective-permute-start(bf16[3,32,1024]{2,1,0:T(8,128)(2,1)S(1)} %get-tuple-element.263), channel_id=1, source_target_pairs={{0,12},{4,8},{8,4},{12,0},{16,28},{20,24},{24,20},{28,16},{1,13},{... | collective-permute-start | bytes 589832 | tf_op jit(solution)/shard_map/ppermute | solution.py:16
  177.7 10.6 %collective-permute-start.49 = (bf16[3,32,1024]{2,1,0:T(8,128)(2,1)S(1)}, bf16[3,32,1024]{2,1,0:T(8,128)(2,1)S(1)}, u32[]{:S(2)}, u32[]{:S(2)}) collective-permute-start(bf16[3,32,1024]{2,1,0:T(8,128)(2,1)S(1)} %get-tuple-element.262), channel_id=1, source_target_pairs={{0,4},{4,0},{8,12},{12,8},{16,20},{20,16},{24,28},{28,24},{1,5},{5... | collective-permute-start | bytes 589832 | tf_op jit(solution)/shard_map/ppermute | solution.py:16
  178.5 10.3 %collective-permute-start.50 = (bf16[3,32,1024]{2,1,0:T(8,128)(2,1)S(1)}, bf16[3,32,1024]{2,1,0:T(8,128)(2,1)S(1)}, u32[]{:S(2)}, u32[]{:S(2)}) collective-permute-start(bf16[3,32,1024]{2,1,0:T(8,128)(2,1)S(1)} %get-tuple-element.261), channel_id=1, source_target_pairs={{0,12},{4,8},{8,4},{12,0},{16,28},{20,24},{24,20},{28,16},{1,13},{... | collective-permute-start | bytes 589832 | tf_op jit(solution)/shard_map/ppermute | solution.py:16
  182.5 7.9 %collective-permute-start.51 = (bf16[3,64,1024]{2,1,0:T(8,128)(2,1)S(1)}, bf16[3,64,1024]{2,1,0:T(8,128)(2,1)S(1)}, u32[]{:S(2)}, u32[]{:S(2)}) collective-permute-start(bf16[3,64,1024]{2,1,0:T(8,128)(2,1)S(1)} %get-tuple-element.202), channel_id=1, source_target_pairs={{0,4},{4,0},{8,12},{12,8},{16,20},{20,16},{24,28},{28,24},{1,5},{5... | collective-permute-start | bytes 1179656 | tf_op jit(solution)/shard_map/ppermute | solution.py:16
  182.7 9.0 %collective-permute-start.52 = (bf16[3,64,1024]{2,1,0:T(8,128)(2,1)S(1)}, bf16[3,64,1024]{2,1,0:T(8,128)(2,1)S(1)}, u32[]{:S(2)}, u32[]{:S(2)}) collective-permute-start(bf16[3,64,1024]{2,1,0:T(8,128)(2,1)S(1)} %get-tuple-element.203), channel_id=1, source_target_pairs={{0,12},{4,8},{8,4},{12,0},{16,28},{20,24},{24,20},{28,16},{1,13},{... | collective-permute-start | bytes 1179656 | tf_op jit(solution)/shard_map/ppermute | solution.py:16
  183.3 8.4 %collective-permute-start.53 = (bf16[1792,512]{1,0:T(8,128)(2,1)S(1)}, bf16[1792,512]{1,0:T(8,128)(2,1)S(1)}, u32[]{:S(2)}, u32[]{:S(2)}) collective-permute-start(bf16[1792,512]{1,0:T(8,128)(2,1)S(1)} %convolution_convert_fusion.2), channel_id=1, source_target_pairs={{0,32},{32,0},{64,96},{96,64},{1,33},{33,1},{65,97},{97,65},{2,34}... | collective-permute-start | bytes 5505032 | tf_op jit(solution)/shard_map/ppermute | solution.py:16
  188.3 21.1 %collective-permute-start.57 = (bf16[512,1792]{1,0:T(8,128)(2,1)S(1)}, bf16[512,1792]{1,0:T(8,128)(2,1)S(1)}, u32[]{:S(2)}, u32[]{:S(2)}) collective-permute-start(bf16[512,1792]{1,0:T(8,128)(2,1)S(1)} %convolution_convert_fusion), channel_id=1, source_target_pairs={{0,32},{32,0},{64,96},{96,64},{1,33},{33,1},{65,97},{97,65},{2,34}... | collective-permute-start | bytes 5505032 | tf_op jit(solution)/shard_map/ppermute | solution.py:16
  191.7 17.7 %collective-permute-start.56 = (bf16[512,1792]{1,0:T(8,128)(2,1)S(1)}, bf16[512,1792]{1,0:T(8,128)(2,1)S(1)}, u32[]{:S(2)}, u32[]{:S(2)}) collective-permute-start(bf16[512,1792]{1,0:T(8,128)(2,1)S(1)} %convolution_convert_fusion.1), channel_id=1, source_target_pairs={{0,32},{32,0},{64,96},{96,64},{1,33},{33,1},{65,97},{97,65},{2,34}... | collective-permute-start | bytes 5505032 | tf_op jit(solution)/shard_map/ppermute | solution.py:16
  192.2 5.7 %collective-permute-start.58 = (bf16[3,16,1024]{2,1,0:T(8,128)(2,1)S(1)}, bf16[3,16,1024]{2,1,0:T(8,128)(2,1)S(1)}, u32[]{:S(2)}, u32[]{:S(2)}) collective-permute-start(bf16[3,16,1024]{2,1,0:T(8,128)(2,1)S(1)} %constant_dynamic-slice_fusion.5), channel_id=1, source_target_pairs={{0,64},{32,96},{64,0},{96,32},{1,65},{33,97},{65,1},{97,33},{2,66}... | collective-permute-start | bytes 294920 | tf_op jit(solution)/shard_map/ppermute | solution.py:16
  193.7 6.4 %collective-permute-start.59 = (bf16[3,16,1024]{2,1,0:T(8,128)(2,1)S(1)}, bf16[3,16,1024]{2,1,0:T(8,128)(2,1)S(1)}, u32[]{:S(2)}, u32[]{:S(2)}) collective-permute-start(bf16[3,16,1024]{2,1,0:T(8,128)(2,1)S(1)} %get-tuple-element.218), channel_id=1, source_target_pairs={{0,16},{4,20},{8,24},{12,28},{16,0},{20,4},{24,8},{28,12},{1,17},{... | collective-permute-start | bytes 294920 | tf_op jit(solution)/shard_map/ppermute | solution.py:16
  194.9 11.1 %collective-permute-start.54 = (bf16[3,64,1024]{2,1,0:T(8,128)(2,1)S(1)}, bf16[3,64,1024]{2,1,0:T(8,128)(2,1)S(1)}, u32[]{:S(2)}, u32[]{:S(2)}) collective-permute-start(bf16[3,64,1024]{2,1,0:T(8,128)(2,1)S(1)} %get-tuple-element.209), channel_id=1, source_target_pairs={{0,4},{4,0},{8,12},{12,8},{16,20},{20,16},{24,28},{28,24},{1,5},{5... | collective-permute-start | bytes 1179656 | tf_op jit(solution)/shard_map/ppermute | solution.py:16
  197.8 11.6 %collective-permute-start.55 = (bf16[3,64,1024]{2,1,0:T(8,128)(2,1)S(1)}, bf16[3,64,1024]{2,1,0:T(8,128)(2,1)S(1)}, u32[]{:S(2)}, u32[]{:S(2)}) collective-permute-start(bf16[3,64,1024]{2,1,0:T(8,128)(2,1)S(1)} %get-tuple-element.210), channel_id=1, source_target_pairs={{0,12},{4,8},{8,4},{12,0},{16,28},{20,24},{24,20},{28,16},{1,13},{... | collective-permute-start | bytes 1179656 | tf_op jit(solution)/shard_map/ppermute | solution.py:16
  200.2 5.8 %collective-permute-start.60 = (bf16[3,16,1024]{2,1,0:T(8,128)(2,1)S(1)}, bf16[3,16,1024]{2,1,0:T(8,128)(2,1)S(1)}, u32[]{:S(2)}, u32[]{:S(2)}) collective-permute-start(bf16[3,16,1024]{2,1,0:T(8,128)(2,1)S(1)} %get-tuple-element.219), channel_id=1, source_target_pairs={{0,80},{4,84},{8,88},{12,92},{16,64},{20,68},{24,72},{28,76},{32,1... | collective-permute-start | bytes 294920 | tf_op jit(solution)/shard_map/ppermute | solution.py:32
  209.7 11.4 %collective-permute-start.61 = (bf16[3,16,1024]{2,1,0:T(8,128)(2,1)S(1)}, bf16[3,16,1024]{2,1,0:T(8,128)(2,1)S(1)}, u32[]{:S(2)}, u32[]{:S(2)}) collective-permute-start(bf16[3,16,1024]{2,1,0:T(8,128)(2,1)S(1)} %constant_dynamic-slice_fusion.2), channel_id=1, source_target_pairs={{0,64},{32,96},{64,0},{96,32},{1,65},{33,97},{65,1},{97,33},{2,66}... | collective-permute-start | bytes 294920 | tf_op jit(solution)/shard_map/ppermute | solution.py:16
  211.3 9.8 %collective-permute-start.62 = (bf16[3,16,1024]{2,1,0:T(8,128)(2,1)S(1)}, bf16[3,16,1024]{2,1,0:T(8,128)(2,1)S(1)}, u32[]{:S(2)}, u32[]{:S(2)}) collective-permute-start(bf16[3,16,1024]{2,1,0:T(8,128)(2,1)S(1)} %get-tuple-element.226), channel_id=1, source_target_pairs={{0,16},{4,20},{8,24},{12,28},{16,0},{20,4},{24,8},{28,12},{1,17},{... | collective-permute-start | bytes 294920 | tf_op jit(solution)/shard_map/ppermute | solution.py:16
  212.2 8.9 %collective-permute-start.63 = (bf16[3,16,1024]{2,1,0:T(8,128)(2,1)S(1)}, bf16[3,16,1024]{2,1,0:T(8,128)(2,1)S(1)}, u32[]{:S(2)}, u32[]{:S(2)}) collective-permute-start(bf16[3,16,1024]{2,1,0:T(8,128)(2,1)S(1)} %get-tuple-element.227), channel_id=1, source_target_pairs={{0,80},{4,84},{8,88},{12,92},{16,64},{20,68},{24,72},{28,76},{32,1... | collective-permute-start | bytes 294920 | tf_op jit(solution)/shard_map/ppermute | solution.py:32
  (14 other events, 130.1 us)
where the time goes:
time: 226 us; the launch traced here: 222 us
  starting transfers between devices  84.8 us (38%)
  waiting for transfers between devices  80.9 us (36%)
  matrix products  33.9 us (15%)
  other arithmetic  14.8 us (7%)
  local copies, waits for them, and re-layouts  5.62 us (2%)
    ppermute x60, starting transfers between devices, swap(): return lax.ppermute(value, axis, [(i, i ^ flip) for i in range(size)])  80 us
    ppermute x60, waiting for transfers between devices, swap(): return lax.ppermute(value, axis, [(i, i ^ flip) for i in range(size)])  78.1 us
    dot_general x15, matrix products, dot(): lax.dot_general(left, right, (dims, ((), ())), preferred_element_type=F32)  18.5 us
    dot_general x3, matrix products, own_plus(): lax.dot_general(left, right, (((0,), (0,)), ((), ())), preferred_element_...  8.57 us
    select_n x23, other arithmetic, either(): return jnp.where(bit == 0, if_zero, if_one)  5.43 us
    ppermute x4, starting transfers between devices, swap_zboth(): lax.ppermute(value, ('depth', 'inw'), [(i, i ^ 20) for i in range(32)])  4.78 us
  transfers between devices with their start and end apart: 64, of which 27 were waited for; matrix products, arithmetic and copies ran while one was open for 18% of the time, Pallas kernels for 0%

commit v1 on v0

--- a/solution.py
+++ b/solution.py
@@ -207,8 +207,9 @@
         hid = (jax.nn.silu(gate_sum) * up_sum).astype(BF16)[None]
         grad_hidden = add(g_part, after(swap_link(g_give, links[2]), hid))
         act = act_grads(grad_hidden, gate_sum, up_sum)
-        hid = doubled(hid, swap_link(hid, links[1]), links[1], bits)
-        act = doubled(act, swap_link(act, links[1]), links[1], bits)
+        both = jnp.concatenate([hid, act], 0)
+        both = doubled(both, swap_link(both, links[1]), links[1], bits)
+        hid, act = both[:1], both[1:]
         hidden.append(doubled(hid, swap_link(hid, links[0]), links[0], bits)[0])
         acts.append(act)
         act_gots.append(swap_link(act, links[0]))

time: 226 us -> 249 us (1.10)
  waiting for transfers between devices: 80.9 us -> 111 us
  starting transfers between devices: 84.8 us -> 77.4 us
    ppermute x60 -> x57, waiting for transfers between devices: 78.1 us -> 108 us  [swap(): return lax.ppermute(value, axis, [(i, i ^ flip) for i in range(size)])]
    ppermute x60 -> x57, starting transfers between devices: 80 us -> 72.7 us  [swap(): return lax.ppermute(value, axis, [(i, i ^ flip) for i in range(size)])]
    select_n x23 -> x17, other arithmetic: 5.43 us -> 5.47 us  [either(): return jnp.where(bit == 0, if_zero, if_one)]
  transfers between devices with their start and end apart: 64 -> 61, of which waited for: 27 -> 27; matrix products, arithmetic and copies ran while one was open for 18% -> 17% of each run, Pallas kernels for 0% -> 0%
where the time goes in v1:
time: 249 us; the launch traced here: 244 us
  waiting for transfers between devices  111 us (45%)
  starting transfers between devices  77.4 us (31%)
  matrix products  33.9 us (14%)
  other arithmetic  14.6 us (6%)
  local copies, waits for them, and re-layouts  5.88 us (2%)
    ppermute x57, waiting for transfers between devices, swap(): return lax.ppermute(value, axis, [(i, i ^ flip) for i in range(size)])  108 us
    ppermute x57, starting transfers between devices, swap(): return lax.ppermute(value, axis, [(i, i ^ flip) for i in range(size)])  72.7 us
    dot_general x15, matrix products, dot(): lax.dot_general(left, right, (dims, ((), ())), preferred_element_type=F32)  18.5 us
    dot_general x3, matrix products, own_plus(): lax.dot_general(left, right, (((0,), (0,)), ((), ())), preferred_element_...  8.57 us
    select_n x17, other arithmetic, either(): return jnp.where(bit == 0, if_zero, if_one)  5.47 us
  transfers between devices with their start and end apart: 61, of which 27 were waited for; matrix products, arithmetic and copies ran while one was open for 17% of the time, Pallas kernels for 0%

profile of v1, /device:TPU:0, one launch (start us, length us, event | category | flops | bytes accessed | tf_op | source)
XLA Modules:
  0.0 244.5 jit_solution(10006671742986853668)
XLA Ops:
  2.2 2.1 collective-permute-start.2
  4.3 3.6 %collective-permute-start.3 = (bf16[3,16,1024]{2,1,0:T(8,128)(2,1)S(1)}, bf16[3,16,1024]{2,1,0:T(8,128)(2,1)S(1)}, u32[]{:S(2)}, u32[]{:S(2)}) collective-permute-start(bf16[3,16,1024]{2,1,0:T(8,128)(2,1)S(1)} %get-tuple-element.124), channel_id=1, source_target_pairs={{0,16},{4,20},{8,24},{12,28},{16,0},{20,4},{24,8},{28,12},{1,17},{... | collective-permute-start | bytes 294920 | tf_op jit(solution)/shard_map/ppermute | solution.py:16
  7.9 4.9 %collective-permute-done.3 = bf16[3,16,1024]{2,1,0:T(8,128)(2,1)S(1)} collective-permute-done((bf16[3,16,1024]{2,1,0:T(8,128)(2,1)S(1)}, bf16[3,16,1024]{2,1,0:T(8,128)(2,1)S(1)}, u32[]{:S(2)}, u32[]{:S(2)}) %collective-permute-start.3) | collective-permute-done | bytes 98336 | tf_op jit(solution)/shard_map/ppermute | solution.py:16
  12.8 1.8 collective-permute-done.4
  14.8 1.6 collective-permute-start.5
  16.4 2.1 collective-permute-start.6
  19.1 1.7 pad_maximum_fusion
  20.9 2.4 collective-permute-done.7
  23.2 1.3 collective-permute-start.8
  24.5 1.7 pad_maximum_fusion.1
  26.3 3.0 %collective-permute-done.8 = bf16[3,16,1024]{2,1,0:T(8,128)(2,1)S(1)} collective-permute-done((bf16[3,16,1024]{2,1,0:T(8,128)(2,1)S(1)}, bf16[3,16,1024]{2,1,0:T(8,128)(2,1)S(1)}, u32[]{:S(2)}, u32[]{:S(2)}) %collective-permute-start.8) | collective-permute-done | bytes 98336 | tf_op jit(solution)/shard_map/ppermute | solution.py:16
  30.9 4.2 %collective-permute-done.10 = bf16[3,32,1024]{2,1,0:T(8,128)(2,1)S(1)} collective-permute-done((bf16[3,32,1024]{2,1,0:T(8,128)(2,1)S(1)}, bf16[3,32,1024]{2,1,0:T(8,128)(2,1)S(1)}, u32[]{:S(2)}, u32[]{:S(2)}) %collective-permute-start.10) | collective-permute-done | bytes 196640 | tf_op jit(solution)/shard_map/ppermute | solution.py:16
  35.1 1.9 collective-permute-done.11
  45.4 1.7 collective-permute-start.18
  47.2 2.3 collective-permute-start.26
  49.6 8.9 %collective-permute-start.34 = (bf16[2,128,1792]{2,1,0:T(8,128)(2,1)S(1)}, bf16[2,128,1792]{2,1,0:T(8,128)(2,1)S(1)}, u32[]{:S(2)}, u32[]{:S(2)}) collective-permute-start(bf16[2,128,1792]{2,1,0:T(8,128)(2,1)S(1)} %pad_maximum_fusion.17), channel_id=1, source_target_pairs={{0,64},{32,96},{64,0},{96,32},{1,65},{33,97},{65,1},{97,33},{2,66}... | collective-permute-start | bytes 2752520 | tf_op jit(solution)/shard_map/ppermute | solution.py:16
  60.1 2.6 %collective-permute-start.16 = (bf16[3,32,1024]{2,1,0:T(8,128)(2,1)S(1)}, bf16[3,32,1024]{2,1,0:T(8,128)(2,1)S(1)}, u32[]{:S(2)}, u32[]{:S(2)}) collective-permute-start(bf16[3,32,1024]{2,1,0:T(8,128)(2,1)S(1)} %slice.219), channel_id=1, source_target_pairs={{0,12},{4,8},{8,4},{12,0},{16,28},{20,24},{24,20},{28,16},{1,13},{... | collective-permute-start | bytes 589832 | tf_op jit(solution)/shard_map/ppermute | solution.py:16
  62.8 2.2 collective-permute-done.15
  65.0 2.0 collective-permute-done.16
  67.1 1.2 convolution_convert_fusion.11
  68.2 1.2 convolution_convert_fusion.8
  71.0 1.2 convolution_convert_fusion.5
  72.2 2.1 collective-permute-start.33
  74.7 2.7 %collective-permute-start.20 = (bf16[2,64,1792]{2,1,0:T(8,128)(2,1)S(1)}, bf16[2,64,1792]{2,1,0:T(8,128)(2,1)S(1)}, u32[]{:S(2)}, u32[]{:S(2)}) collective-permute-start(bf16[2,64,1792]{2,1,0:T(8,128)(2,1)S(1)} %pad_maximum_fusion.25), channel_id=1, source_target_pairs={{0,3},{1,2},{2,1},{3,0},{4,7},{5,6},{6,5},{7,4},{8,11},{9,10},{10,... | collective-permute-start | bytes 1376264 | tf_op jit(solution)/shard_map/ppermute | solution.py:16
  77.7 4.2 %collective-permute-done.34 = bf16[2,128,1792]{2,1,0:T(8,128)(2,1)S(1)} collective-permute-done((bf16[2,128,1792]{2,1,0:T(8,128)(2,1)S(1)}, bf16[2,128,1792]{2,1,0:T(8,128)(2,1)S(1)}, u32[]{:S(2)}, u32[]{:S(2)}) %collective-permute-start.34) | collective-permute-done | bytes 917536 | tf_op jit(solution)/shard_map/ppermute | solution.py:16
  83.1 1.9 collective-permute-done.25
  85.7 5.9 %collective-permute-done.33 = bf16[1,128,1792]{2,1,0:T(8,128)(2,1)S(1)} collective-permute-done((bf16[1,128,1792]{2,1,0:T(8,128)(2,1)S(1)}, bf16[1,128,1792]{2,1,0:T(8,128)(2,1)S(1)}, u32[]{:S(2)}, u32[]{:S(2)}) %collective-permute-start.33) | collective-permute-done | bytes 458784 | tf_op jit(solution)/shard_map/ppermute | solution.py:16
  93.1 1.8 collective-permute-start.21
  94.9 6.6 %collective-permute-done.28 = bf16[2,64,1792]{2,1,0:T(8,128)(2,1)S(1)} collective-permute-done((bf16[2,64,1792]{2,1,0:T(8,128)(2,1)S(1)}, bf16[2,64,1792]{2,1,0:T(8,128)(2,1)S(1)}, u32[]{:S(2)}, u32[]{:S(2)}) %collective-permute-start.28) | collective-permute-done | bytes 458784 | tf_op jit(solution)/shard_map/ppermute | solution.py:16
  101.7 4.7 %collective-permute-done.27 = bf16[1,64,1792]{2,1,0:T(8,128)(2,1)S(1)} collective-permute-done((bf16[1,64,1792]{2,1,0:T(8,128)(2,1)S(1)}, bf16[1,64,1792]{2,1,0:T(8,128)(2,1)S(1)}, u32[]{:S(2)}, u32[]{:S(2)}) %collective-permute-start.27) | collective-permute-done | bytes 229408 | tf_op jit(solution)/shard_map/ppermute | solution.py:16
  108.2 1.2 collective-permute-start.29
  109.4 6.9 %collective-permute-done.22 = bf16[64,1792]{1,0:T(8,128)(2,1)S(1)} collective-permute-done((bf16[64,1792]{1,0:T(8,128)(2,1)S(1)}, bf16[64,1792]{1,0:T(8,128)(2,1)S(1)}, u32[]{:S(2)}, u32[]{:S(2)}) %collective-permute-start.22) | collective-permute-done | bytes 229408 | tf_op jit(solution)/shard_map/ppermute | solution.py:16
  117.9 2.3 collective-permute-start.23
  120.2 10.8 %collective-permute-done.37 = bf16[2,64,1792]{2,1,0:T(8,128)(2,1)S(1)} collective-permute-done((bf16[2,64,1792]{2,1,0:T(8,128)(2,1)S(1)}, bf16[2,64,1792]{2,1,0:T(8,128)(2,1)S(1)}, u32[]{:S(2)}, u32[]{:S(2)}) %collective-permute-start.37) | collective-permute-done | bytes 458784 | tf_op jit(solution)/shard_map/ppermute | solution.py:16
  132.8 15.3 %collective-permute-done.39 = bf16[3,64,1792]{2,1,0:T(8,128)(2,1)S(1)} collective-permute-done((bf16[3,64,1792]{2,1,0:T(8,128)(2,1)S(1)}, bf16[3,64,1792]{2,1,0:T(8,128)(2,1)S(1)}, u32[]{:S(2)}, u32[]{:S(2)}) %collective-permute-start.39) | collective-permute-done | bytes 688160 | tf_op jit(solution)/shard_map/ppermute | solution.py:16
  149.7 3.0 %collective-permute-start.24 = (bf16[2,128,1792]{2,1,0:T(8,128)(2,1)S(1)}, bf16[2,128,1792]{2,1,0:T(8,128)(2,1)S(1)}, u32[]{:S(2)}, u32[]{:S(2)}) collective-permute-start(bf16[2,128,1792]{2,1,0:T(8,128)(2,1)S(1)} %slice.284), channel_id=1, source_target_pairs={{0,1},{1,0},{2,3},{3,2},{4,5},{5,4},{6,7},{7,6},{8,9},{9,8},{10,11... | collective-permute-start | bytes 2752520 | tf_op jit(solution)/shard_map/ppermute | solution.py:16
  152.7 2.0 collective-permute-start.43
  154.8 3.2 %collective-permute-start.42 = (bf16[1,128,1792]{2,1,0:T(8,128)(2,1)S(1)}, bf16[1,128,1792]{2,1,0:T(8,128)(2,1)S(1)}, u32[]{:S(2)}, u32[]{:S(2)}) collective-permute-start(bf16[1,128,1792]{2,1,0:T(8,128)(2,1)S(1)} %get-tuple-element.268), channel_id=1, source_target_pairs={{0,3},{1,2},{2,1},{3,0},{4,7},{5,6},{6,5},{7,4},{8,11},{9,10},{10,... | collective-permute-start | bytes 1376264 | tf_op jit(solution)/shard_map/ppermute | solution.py:16
  158.1 14.9 %collective-permute-done.43 = bf16[1,128,1792]{2,1,0:T(8,128)(2,1)S(1)} collective-permute-done((bf16[1,128,1792]{2,1,0:T(8,128)(2,1)S(1)}, bf16[1,128,1792]{2,1,0:T(8,128)(2,1)S(1)}, u32[]{:S(2)}, u32[]{:S(2)}) %collective-permute-start.43) | collective-permute-done | bytes 458784 | tf_op jit(solution)/shard_map/ppermute | solution.py:16
  173.0 2.0 collective-permute-start.41
  176.5 1.1 fusion.4
  177.7 3.8 %collective-permute-done.41 = bf16[1,128,1792]{2,1,0:T(8,128)(2,1)S(1)} collective-permute-done((bf16[1,128,1792]{2,1,0:T(8,128)(2,1)S(1)}, bf16[1,128,1792]{2,1,0:T(8,128)(2,1)S(1)}, u32[]{:S(2)}, u32[]{:S(2)}) %collective-permute-start.41) | collective-permute-done | bytes 458784 | tf_op jit(solution)/shard_map/ppermute | solution.py:16
  183.6 1.6 collective-permute-start.45
  185.2 1.6 convolution_convert_fusion.2
  186.8 1.8 collective-permute-done.44
  188.6 2.3 collective-permute-done.45
  192.9 1.9 copy-done.3
  194.8 1.1 fusion.6
  203.6 1.4 collective-permute-start.48
  205.0 2.1 collective-permute-start.49
  207.5 1.3 copy-done.13
  208.7 1.6 convolution_convert_fusion.1
  210.4 1.6 convolution_convert_fusion
  212.6 1.4 collective-permute-done.49
  214.8 2.3 collective-permute-start.56
  217.4 2.7 %collective-permute-done.55 = bf16[3,16,1024]{2,1,0:T(8,128)(2,1)S(1)} collective-permute-done((bf16[3,16,1024]{2,1,0:T(8,128)(2,1)S(1)}, bf16[3,16,1024]{2,1,0:T(8,128)(2,1)S(1)}, u32[]{:S(2)}, u32[]{:S(2)}) %collective-permute-start.55) | collective-permute-done | bytes 98336 | tf_op jit(solution)/shard_map/ppermute | solution.py:16
  220.1 2.1 collective-permute-start.52
  222.4 2.1 collective-permute-start.57
  224.5 2.9 %add_convert_fusion.2 = bf16[1792,512]{1,0:T(8,128)(2,1)} fusion(bf16[1792,512]{1,0:T(8,128)(2,1)S(1)} %collective-permute-done.50, bf16[256,1792]{1,0:T(8,128)(2,1)S(1)} %maximum_select_fusion.8, bf16[256,1792]{1,0:T(8,128)(2,1)S(1)} %maximum_select_fusion.7, bf16[256,1792]{1,0:T(8,128)(2,1)S(1)} %maximum_select_fusion.6, bf16[768,1024]{1,0:T(8,128)(2,1)S(1)} %bitcast.333), kind=kOutput, calls=%fused_computation.5 | convolution fusion | flops 1420296192 | bytes 7208960 | tf_op jit(solution)/shard_map/dot_general | solution.py:232
  228.4 3.3 %collective-permute-done.52 = bf16[3,64,1024]{2,1,0:T(8,128)(2,1)S(1)} collective-permute-done((bf16[3,64,1024]{2,1,0:T(8,128)(2,1)S(1)}, bf16[3,64,1024]{2,1,0:T(8,128)(2,1)S(1)}, u32[]{:S(2)}, u32[]{:S(2)}) %collective-permute-start.52) | collective-permute-done | bytes 393248 | tf_op jit(solution)/shard_map/ppermute | solution.py:16
  232.4 2.3 collective-permute-start.59
  234.7 2.1 collective-permute-start.60
  236.8 2.9 %add_convert_fusion.1 = bf16[512,1792]{1,0:T(8,128)(2,1)} fusion(bf16[512,1792]{1,0:T(8,128)(2,1)S(1)} %collective-permute-done.53, bf16[256,1792]{1,0:T(8,128)(2,1)S(1)} %get-tuple-element.252, bf16[256,1792]{1,0:T(8,128)(2,1)S(1)} %get-tuple-element.250, bf16[256,1792]{1,0:T(8,128)(2,1)S(1)} %get-tuple-element.248, bf16[768,1024]{1,0:T(8,128)(2,1)S(1)} %bitcast.336), kind=kOutput, calls=%fused_computation.4 | convolution fusion | flops 1420296192 | bytes 7208960 | tf_op jit(solution)/shard_map/dot_general | solution.py:232
  239.6 2.9 %add_convert_fusion = bf16[512,1792]{1,0:T(8,128)(2,1)} fusion(bf16[512,1792]{1,0:T(8,128)(2,1)S(1)} %collective-permute-done.54, bf16[256,1792]{1,0:T(8,128)(2,1)S(1)} %get-tuple-element.251, bf16[256,1792]{1,0:T(8,128)(2,1)S(1)} %get-tuple-element.249, bf16[256,1792]{1,0:T(8,128)(2,1)S(1)} %get-tuple-element.247, bf16[768,1024]{1,0:T(8,128)(2,1)S(1)} %bitcast.337), kind=kOutput, calls=%fused_computation.3 | convolution fusion | flops 1420296192 | bytes 7208960 | tf_op jit(solution)/shard_map/dot_general | solution.py:232
  (235 shorter events, 45.2 us)
Async XLA Ops:
  0.6 18.5 %copy-start.6 = (bf16[512,1792]{1,0:T(8,128)(2,1)S(1)}, bf16[512,1792]{1,0:T(8,128)(2,1)}, u32[]{:S(2)}) copy-start(bf16[512,1792]{1,0:T(8,128)(2,1)} %param.6) | copy-start | bytes 5505028
  0.7 14.0 %collective-permute-start = (bf16[512,1792]{1,0:T(8,128)(2,1)}, bf16[512,1792]{1,0:T(8,128)(2,1)}, u32[]{:S(2)}, u32[]{:S(2)}) collective-permute-start(bf16[512,1792]{1,0:T(8,128)(2,1)} %param.6), channel_id=1, source_target_pairs={{0,32},{32,0},{64,96},{96,64},{1,33},{33,1},{65,97},{97,65},{2,34}... | collective-permute-start | bytes 5505032 | tf_op jit(solution)/shard_map/ppermute | solution.py:16
  0.7 13.9 %collective-permute-start.1 = (bf16[512,1792]{1,0:T(8,128)(2,1)}, bf16[512,1792]{1,0:T(8,128)(2,1)}, u32[]{:S(2)}, u32[]{:S(2)}) collective-permute-start(bf16[512,1792]{1,0:T(8,128)(2,1)} %param.7), channel_id=1, source_target_pairs={{0,32},{32,0},{64,96},{96,64},{1,33},{33,1},{65,97},{97,65},{2,34}... | collective-permute-start | bytes 5505032 | tf_op jit(solution)/shard_map/ppermute | solution.py:16
  2.2 5.7 %collective-permute-start.2 = (bf16[3,16,1024]{2,1,0:T(8,128)(2,1)S(1)}, bf16[3,16,1024]{2,1,0:T(8,128)(2,1)S(1)}, u32[]{:S(2)}, u32[]{:S(2)}) collective-permute-start(bf16[3,16,1024]{2,1,0:T(8,128)(2,1)S(1)} %get-tuple-element.125), channel_id=1, source_target_pairs={{0,64},{32,96},{64,0},{96,32},{1,65},{33,97},{65,1},{97,33},{2,66}... | collective-permute-start | bytes 294920 | tf_op jit(solution)/shard_map/ppermute | solution.py:16
  4.3 8.5 %collective-permute-start.3 = (bf16[3,16,1024]{2,1,0:T(8,128)(2,1)S(1)}, bf16[3,16,1024]{2,1,0:T(8,128)(2,1)S(1)}, u32[]{:S(2)}, u32[]{:S(2)}) collective-permute-start(bf16[3,16,1024]{2,1,0:T(8,128)(2,1)S(1)} %get-tuple-element.124), channel_id=1, source_target_pairs={{0,16},{4,20},{8,24},{12,28},{16,0},{20,4},{24,8},{28,12},{1,17},{... | collective-permute-start | bytes 294920 | tf_op jit(solution)/shard_map/ppermute | solution.py:16
  7.9 6.8 %collective-permute-start.4 = (bf16[3,16,1024]{2,1,0:T(8,128)(2,1)S(1)}, bf16[3,16,1024]{2,1,0:T(8,128)(2,1)S(1)}, u32[]{:S(2)}, u32[]{:S(2)}) collective-permute-start(bf16[3,16,1024]{2,1,0:T(8,128)(2,1)S(1)} %get-tuple-element.125), channel_id=1, source_target_pairs={{0,80},{4,84},{8,88},{12,92},{16,64},{20,68},{24,72},{28,76},{32,1... | collective-permute-start | bytes 294920 | tf_op jit(solution)/shard_map/ppermute | solution.py:32
  7.9 29.2 %collective-permute-start.12 = (bf16[1792,512]{1,0:T(8,128)(2,1)}, bf16[1792,512]{1,0:T(8,128)(2,1)S(1)}, u32[]{:S(2)}, u32[]{:S(2)}) collective-permute-start(bf16[1792,512]{1,0:T(8,128)(2,1)} %param.8), channel_id=1, source_target_pairs={{0,32},{32,0},{64,96},{96,64},{1,33},{33,1},{65,97},{97,65},{2,34}... | collective-permute-start | bytes 5505032 | tf_op jit(solution)/shard_map/ppermute | solution.py:16
  14.8 14.6 %collective-permute-start.5 = (bf16[3,64,1024]{2,1,0:T(8,128)(2,1)S(1)}, bf16[3,64,1024]{2,1,0:T(8,128)(2,1)S(1)}, u32[]{:S(2)}, u32[]{:S(2)}) collective-permute-start(bf16[3,64,1024]{2,1,0:T(8,128)(2,1)S(1)} %pad_maximum_fusion.33), channel_id=1, source_target_pairs={{0,4},{4,0},{8,12},{12,8},{16,20},{20,16},{24,28},{28,24},{1,5},{5... | collective-permute-start | bytes 1179656 | tf_op jit(solution)/shard_map/ppermute | solution.py:16
  16.4 13.0 %collective-permute-start.6 = (bf16[3,64,1024]{2,1,0:T(8,128)(2,1)S(1)}, bf16[3,64,1024]{2,1,0:T(8,128)(2,1)S(1)}, u32[]{:S(2)}, u32[]{:S(2)}) collective-permute-start(bf16[3,64,1024]{2,1,0:T(8,128)(2,1)S(1)} %pad_maximum_fusion.33), channel_id=1, source_target_pairs={{0,12},{4,8},{8,4},{12,0},{16,28},{20,24},{24,20},{28,16},{1,13},{... | collective-permute-start | bytes 1179656 | tf_op jit(solution)/shard_map/ppermute | solution.py:16
  18.5 4.7 %collective-permute-start.7 = (bf16[3,16,1024]{2,1,0:T(8,128)(2,1)S(1)}, bf16[3,16,1024]{2,1,0:T(8,128)(2,1)S(1)}, u32[]{:S(2)}, u32[]{:S(2)}) collective-permute-start(bf16[3,16,1024]{2,1,0:T(8,128)(2,1)S(1)} %pad_maximum_fusion.42), channel_id=1, source_target_pairs={{0,64},{32,96},{64,0},{96,32},{1,65},{33,97},{65,1},{97,33},{2,66}... | collective-permute-start | bytes 294920 | tf_op jit(solution)/shard_map/ppermute | solution.py:16
  18.6 10.7 %collective-permute-start.9 = (bf16[3,16,1024]{2,1,0:T(8,128)(2,1)S(1)}, bf16[3,16,1024]{2,1,0:T(8,128)(2,1)S(1)}, u32[]{:S(2)}, u32[]{:S(2)}) collective-permute-start(bf16[3,16,1024]{2,1,0:T(8,128)(2,1)S(1)} %pad_maximum_fusion.42), channel_id=1, source_target_pairs={{0,80},{4,84},{8,88},{12,92},{16,64},{20,68},{24,72},{28,76},{32,1... | collective-permute-start | bytes 294920 | tf_op jit(solution)/shard_map/ppermute | solution.py:32
  20.8 23.2 %copy-start = (bf16[1024,1792]{1,0:T(8,128)(2,1)}, bf16[1024,1792]{1,0:T(8,128)(2,1)S(1)}, u32[]{:S(2)}) copy-start(bf16[1024,1792]{1,0:T(8,128)(2,1)S(1)} %pad_maximum_fusion) | copy-start | bytes 11010052
  23.2 6.1 %collective-permute-start.8 = (bf16[3,16,1024]{2,1,0:T(8,128)(2,1)S(1)}, bf16[3,16,1024]{2,1,0:T(8,128)(2,1)S(1)}, u32[]{:S(2)}, u32[]{:S(2)}) collective-permute-start(bf16[3,16,1024]{2,1,0:T(8,128)(2,1)S(1)} %pad_maximum_fusion.41), channel_id=1, source_target_pairs={{0,16},{4,20},{8,24},{12,28},{16,0},{20,4},{24,8},{28,12},{1,17},{... | collective-permute-start | bytes 294920 | tf_op jit(solution)/shard_map/ppermute | solution.py:16
  29.4 5.7 %collective-permute-start.10 = (bf16[3,32,1024]{2,1,0:T(8,128)(2,1)S(1)}, bf16[3,32,1024]{2,1,0:T(8,128)(2,1)S(1)}, u32[]{:S(2)}, u32[]{:S(2)}) collective-permute-start(bf16[3,32,1024]{2,1,0:T(8,128)(2,1)S(1)} %slice.216), channel_id=1, source_target_pairs={{0,4},{4,0},{8,12},{12,8},{16,20},{20,16},{24,28},{28,24},{1,5},{5... | collective-permute-start | bytes 589832 | tf_op jit(solution)/shard_map/ppermute | solution.py:16
  30.1 7.0 %collective-permute-start.11 = (bf16[3,32,1024]{2,1,0:T(8,128)(2,1)S(1)}, bf16[3,32,1024]{2,1,0:T(8,128)(2,1)S(1)}, u32[]{:S(2)}, u32[]{:S(2)}) collective-permute-start(bf16[3,32,1024]{2,1,0:T(8,128)(2,1)S(1)} %slice.217), channel_id=1, source_target_pairs={{0,12},{4,8},{8,4},{12,0},{16,28},{20,24},{24,20},{28,16},{1,13},{... | collective-permute-start | bytes 589832 | tf_op jit(solution)/shard_map/ppermute | solution.py:16
  37.1 22.1 %collective-permute-start.13 = (bf16[3,64,1024]{2,1,0:T(8,128)(2,1)S(1)}, bf16[3,64,1024]{2,1,0:T(8,128)(2,1)S(1)}, u32[]{:S(2)}, u32[]{:S(2)}) collective-permute-start(bf16[3,64,1024]{2,1,0:T(8,128)(2,1)S(1)} %pad_maximum_fusion.34), channel_id=1, source_target_pairs={{0,4},{4,0},{8,12},{12,8},{16,20},{20,16},{24,28},{28,24},{1,5},{5... | collective-permute-start | bytes 1179656 | tf_op jit(solution)/shard_map/ppermute | solution.py:16
  37.2 22.0 %collective-permute-start.14 = (bf16[3,64,1024]{2,1,0:T(8,128)(2,1)S(1)}, bf16[3,64,1024]{2,1,0:T(8,128)(2,1)S(1)}, u32[]{:S(2)}, u32[]{:S(2)}) collective-permute-start(bf16[3,64,1024]{2,1,0:T(8,128)(2,1)S(1)} %pad_maximum_fusion.34), channel_id=1, source_target_pairs={{0,12},{4,8},{8,4},{12,0},{16,28},{20,24},{24,20},{28,16},{1,13},{... | collective-permute-start | bytes 1179656 | tf_op jit(solution)/shard_map/ppermute | solution.py:16
  45.4 26.8 %collective-permute-start.18 = (bf16[2,128,1792]{2,1,0:T(8,128)(2,1)S(1)}, bf16[2,128,1792]{2,1,0:T(8,128)(2,1)S(1)}, u32[]{:S(2)}, u32[]{:S(2)}) collective-permute-start(bf16[2,128,1792]{2,1,0:T(8,128)(2,1)S(1)} %pad_maximum_fusion.15), channel_id=1, source_target_pairs={{0,1},{1,0},{2,3},{3,2},{4,5},{5,4},{6,7},{7,6},{8,9},{9,8},{10,11... | collective-permute-start | bytes 2752520 | tf_op jit(solution)/shard_map/ppermute | solution.py:16
  47.2 27.4 %collective-permute-start.26 = (bf16[2,128,1792]{2,1,0:T(8,128)(2,1)S(1)}, bf16[2,128,1792]{2,1,0:T(8,128)(2,1)S(1)}, u32[]{:S(2)}, u32[]{:S(2)}) collective-permute-start(bf16[2,128,1792]{2,1,0:T(8,128)(2,1)S(1)} %pad_maximum_fusion.16), channel_id=1, source_target_pairs={{0,3},{1,2},{2,1},{3,0},{4,7},{5,6},{6,5},{7,4},{8,11},{9,10},{10,... | collective-permute-start | bytes 2752520 | tf_op jit(solution)/shard_map/ppermute | solution.py:16
  49.6 32.2 %collective-permute-start.34 = (bf16[2,128,1792]{2,1,0:T(8,128)(2,1)S(1)}, bf16[2,128,1792]{2,1,0:T(8,128)(2,1)S(1)}, u32[]{:S(2)}, u32[]{:S(2)}) collective-permute-start(bf16[2,128,1792]{2,1,0:T(8,128)(2,1)S(1)} %pad_maximum_fusion.17), channel_id=1, source_target_pairs={{0,64},{32,96},{64,0},{96,32},{1,65},{33,97},{65,1},{97,33},{2,66}... | collective-permute-start | bytes 2752520 | tf_op jit(solution)/shard_map/ppermute | solution.py:16
  59.3 5.7 %collective-permute-start.15 = (bf16[3,32,1024]{2,1,0:T(8,128)(2,1)S(1)}, bf16[3,32,1024]{2,1,0:T(8,128)(2,1)S(1)}, u32[]{:S(2)}, u32[]{:S(2)}) collective-permute-start(bf16[3,32,1024]{2,1,0:T(8,128)(2,1)S(1)} %slice.218), channel_id=1, source_target_pairs={{0,4},{4,0},{8,12},{12,8},{16,20},{20,16},{24,28},{28,24},{1,5},{5... | collective-permute-start | bytes 589832 | tf_op jit(solution)/shard_map/ppermute | solution.py:16
  60.1 6.9 %collective-permute-start.16 = (bf16[3,32,1024]{2,1,0:T(8,128)(2,1)S(1)}, bf16[3,32,1024]{2,1,0:T(8,128)(2,1)S(1)}, u32[]{:S(2)}, u32[]{:S(2)}) collective-permute-start(bf16[3,32,1024]{2,1,0:T(8,128)(2,1)S(1)} %slice.219), channel_id=1, source_target_pairs={{0,12},{4,8},{8,4},{12,0},{16,28},{20,24},{24,20},{28,16},{1,13},{... | collective-permute-start | bytes 589832 | tf_op jit(solution)/shard_map/ppermute | solution.py:16
  69.5 12.7 %collective-permute-start.17 = (bf16[1,128,1792]{2,1,0:T(8,128)(2,1)S(1)}, bf16[1,128,1792]{2,1,0:T(8,128)(2,1)S(1)}, u32[]{:S(2)}, u32[]{:S(2)}) collective-permute-start(bf16[1,128,1792]{2,1,0:T(8,128)(2,1)S(1)} %dynamic-slice_bitcast_fusion.8), channel_id=1, source_target_pairs={{0,1},{1,0},{2,3},{3,2},{4,5},{5,4},{6,7},{7,6},{8,9},{9,8},{10,11... | collective-permute-start | bytes 1376264 | tf_op jit(solution)/shard_map/ppermute | solution.py:16
  70.3 14.7 %collective-permute-start.25 = (bf16[1,128,1792]{2,1,0:T(8,128)(2,1)S(1)}, bf16[1,128,1792]{2,1,0:T(8,128)(2,1)S(1)}, u32[]{:S(2)}, u32[]{:S(2)}) collective-permute-start(bf16[1,128,1792]{2,1,0:T(8,128)(2,1)S(1)} %dynamic-slice_bitcast_fusion.5), channel_id=1, source_target_pairs={{0,3},{1,2},{2,1},{3,0},{4,7},{5,6},{6,5},{7,4},{8,11},{9,10},{10,... | collective-permute-start | bytes 1376264 | tf_op jit(solution)/shard_map/ppermute | solution.py:16
  72.2 19.5 %collective-permute-start.33 = (bf16[1,128,1792]{2,1,0:T(8,128)(2,1)S(1)}, bf16[1,128,1792]{2,1,0:T(8,128)(2,1)S(1)}, u32[]{:S(2)}, u32[]{:S(2)}) collective-permute-start(bf16[1,128,1792]{2,1,0:T(8,128)(2,1)S(1)} %dynamic-slice_bitcast_fusion.2), channel_id=1, source_target_pairs={{0,64},{32,96},{64,0},{96,32},{1,65},{33,97},{65,1},{97,33},{2,66}... | collective-permute-start | bytes 1376264 | tf_op jit(solution)/shard_map/ppermute | solution.py:16
  74.7 17.2 %collective-permute-start.20 = (bf16[2,64,1792]{2,1,0:T(8,128)(2,1)S(1)}, bf16[2,64,1792]{2,1,0:T(8,128)(2,1)S(1)}, u32[]{:S(2)}, u32[]{:S(2)}) collective-permute-start(bf16[2,64,1792]{2,1,0:T(8,128)(2,1)S(1)} %pad_maximum_fusion.25), channel_id=1, source_target_pairs={{0,3},{1,2},{2,1},{3,0},{4,7},{5,6},{6,5},{7,4},{8,11},{9,10},{10,... | collective-permute-start | bytes 1376264 | tf_op jit(solution)/shard_map/ppermute | solution.py:16
  81.8 19.7 %collective-permute-start.28 = (bf16[2,64,1792]{2,1,0:T(8,128)(2,1)S(1)}, bf16[2,64,1792]{2,1,0:T(8,128)(2,1)S(1)}, u32[]{:S(2)}, u32[]{:S(2)}) collective-permute-start(bf16[2,64,1792]{2,1,0:T(8,128)(2,1)S(1)} %pad_maximum_fusion.27), channel_id=1, source_target_pairs={{0,64},{32,96},{64,0},{96,32},{1,65},{33,97},{65,1},{97,33},{2,66}... | collective-permute-start | bytes 1376264 | tf_op jit(solution)/shard_map/ppermute | solution.py:16
  82.2 25.0 %collective-permute-start.36 = (bf16[2,64,1792]{2,1,0:T(8,128)(2,1)S(1)}, bf16[2,64,1792]{2,1,0:T(8,128)(2,1)S(1)}, u32[]{:S(2)}, u32[]{:S(2)}) collective-permute-start(bf16[2,64,1792]{2,1,0:T(8,128)(2,1)S(1)} %pad_maximum_fusion.29), channel_id=1, source_target_pairs={{0,1},{1,0},{2,3},{3,2},{4,5},{5,4},{6,7},{7,6},{8,9},{9,8},{10,11... | collective-permute-start | bytes 1376264 | tf_op jit(solution)/shard_map/ppermute | solution.py:16
  85.0 8.0 %collective-permute-start.19 = (bf16[1,64,1792]{2,1,0:T(8,128)(2,1)S(1)}, bf16[1,64,1792]{2,1,0:T(8,128)(2,1)S(1)}, u32[]{:S(2)}, u32[]{:S(2)}) collective-permute-start(bf16[1,64,1792]{2,1,0:T(8,128)(2,1)S(1)} %dynamic-slice_bitcast_fusion.17), channel_id=1, source_target_pairs={{0,3},{1,2},{2,1},{3,0},{4,7},{5,6},{6,5},{7,4},{8,11},{9,10},{10,... | collective-permute-start | bytes 688136 | tf_op jit(solution)/shard_map/ppermute | solution.py:16
  91.7 14.7 %collective-permute-start.27 = (bf16[1,64,1792]{2,1,0:T(8,128)(2,1)S(1)}, bf16[1,64,1792]{2,1,0:T(8,128)(2,1)S(1)}, u32[]{:S(2)}, u32[]{:S(2)}) collective-permute-start(bf16[1,64,1792]{2,1,0:T(8,128)(2,1)S(1)} %dynamic-slice_bitcast_fusion.14), channel_id=1, source_target_pairs={{0,64},{32,96},{64,0},{96,32},{1,65},{33,97},{65,1},{97,33},{2,66}... | collective-permute-start | bytes 688136 | tf_op jit(solution)/shard_map/ppermute | solution.py:16
  91.8 15.6 %collective-permute-start.35 = (bf16[1,64,1792]{2,1,0:T(8,128)(2,1)S(1)}, bf16[1,64,1792]{2,1,0:T(8,128)(2,1)S(1)}, u32[]{:S(2)}, u32[]{:S(2)}) collective-permute-start(bf16[1,64,1792]{2,1,0:T(8,128)(2,1)S(1)} %dynamic-slice_bitcast_fusion.11), channel_id=1, source_target_pairs={{0,1},{1,0},{2,3},{3,2},{4,5},{5,4},{6,7},{7,6},{8,9},{9,8},{10,11... | collective-permute-start | bytes 688136 | tf_op jit(solution)/shard_map/ppermute | solution.py:16
  93.1 24.3 %collective-permute-start.21 = (bf16[2,64,1792]{2,1,0:T(8,128)(2,1)S(1)}, bf16[2,64,1792]{2,1,0:T(8,128)(2,1)S(1)}, u32[]{:S(2)}, u32[]{:S(2)}) collective-permute-start(bf16[2,64,1792]{2,1,0:T(8,128)(2,1)S(1)} %pad_maximum_fusion.26), channel_id=1, source_target_pairs={{0,64},{32,96},{64,0},{96,32},{1,65},{33,97},{65,1},{97,33},{2,66}... | collective-permute-start | bytes 1376264 | tf_op jit(solution)/shard_map/ppermute | solution.py:16
  101.5 14.8 %collective-permute-start.22 = (bf16[64,1792]{1,0:T(8,128)(2,1)S(1)}, bf16[64,1792]{1,0:T(8,128)(2,1)S(1)}, u32[]{:S(2)}, u32[]{:S(2)}) collective-permute-start(bf16[64,1792]{1,0:T(8,128)(2,1)S(1)} %fusion.49), channel_id=1, source_target_pairs={{0,64},{32,96},{64,0},{96,32},{1,65},{33,97},{65,1},{97,33},{2,66}... | collective-permute-start | bytes 688136 | tf_op jit(solution)/shard_map/ppermute | solution.py:16
  106.5 10.9 %collective-permute-start.30 = (bf16[64,1792]{1,0:T(8,128)(2,1)S(1)}, bf16[64,1792]{1,0:T(8,128)(2,1)S(1)}, u32[]{:S(2)}, u32[]{:S(2)}) collective-permute-start(bf16[64,1792]{1,0:T(8,128)(2,1)S(1)} %fusion.46), channel_id=1, source_target_pairs={{0,1},{1,0},{2,3},{3,2},{4,5},{5,4},{6,7},{7,6},{8,9},{9,8},{10,11... | collective-permute-start | bytes 688136 | tf_op jit(solution)/shard_map/ppermute | solution.py:16
  107.5 9.9 %collective-permute-start.38 = (bf16[64,1792]{1,0:T(8,128)(2,1)S(1)}, bf16[64,1792]{1,0:T(8,128)(2,1)S(1)}, u32[]{:S(2)}, u32[]{:S(2)}) collective-permute-start(bf16[64,1792]{1,0:T(8,128)(2,1)S(1)} %fusion.43), channel_id=1, source_target_pairs={{0,3},{1,2},{2,1},{3,0},{4,7},{5,6},{6,5},{7,4},{8,11},{9,10},{10,... | collective-permute-start | bytes 688136 | tf_op jit(solution)/shard_map/ppermute | solution.py:16
  108.2 12.0 %collective-permute-start.29 = (bf16[2,64,1792]{2,1,0:T(8,128)(2,1)S(1)}, bf16[2,64,1792]{2,1,0:T(8,128)(2,1)S(1)}, u32[]{:S(2)}, u32[]{:S(2)}) collective-permute-start(bf16[2,64,1792]{2,1,0:T(8,128)(2,1)S(1)} %pad_maximum_fusion.28), channel_id=1, source_target_pairs={{0,1},{1,0},{2,3},{3,2},{4,5},{5,4},{6,7},{7,6},{8,9},{9,8},{10,11... | collective-permute-start | bytes 1376264 | tf_op jit(solution)/shard_map/ppermute | solution.py:16
  116.3 14.7 %collective-permute-start.37 = (bf16[2,64,1792]{2,1,0:T(8,128)(2,1)S(1)}, bf16[2,64,1792]{2,1,0:T(8,128)(2,1)S(1)}, u32[]{:S(2)}, u32[]{:S(2)}) collective-permute-start(bf16[2,64,1792]{2,1,0:T(8,128)(2,1)S(1)} %pad_maximum_fusion.30), channel_id=1, source_target_pairs={{0,3},{1,2},{2,1},{3,0},{4,7},{5,6},{6,5},{7,4},{8,11},{9,10},{10,... | collective-permute-start | bytes 1376264 | tf_op jit(solution)/shard_map/ppermute | solution.py:16
  117.9 31.3 %collective-permute-start.23 = (bf16[3,64,1792]{2,1,0:T(8,128)(2,1)S(1)}, bf16[3,64,1792]{2,1,0:T(8,128)(2,1)S(1)}, u32[]{:S(2)}, u32[]{:S(2)}) collective-permute-start(bf16[3,64,1792]{2,1,0:T(8,128)(2,1)S(1)} %pad_maximum_fusion.22), channel_id=1, source_target_pairs={{0,3},{1,2},{2,1},{3,0},{4,7},{5,6},{6,5},{7,4},{8,11},{9,10},{10,... | collective-permute-start | bytes 2064392 | tf_op jit(solution)/shard_map/ppermute | solution.py:16
  131.6 16.6 %collective-permute-start.39 = (bf16[3,64,1792]{2,1,0:T(8,128)(2,1)S(1)}, bf16[3,64,1792]{2,1,0:T(8,128)(2,1)S(1)}, u32[]{:S(2)}, u32[]{:S(2)}) collective-permute-start(bf16[3,64,1792]{2,1,0:T(8,128)(2,1)S(1)} %pad_maximum_fusion.24), channel_id=1, source_target_pairs={{0,1},{1,0},{2,3},{3,2},{4,5},{5,4},{6,7},{7,6},{8,9},{9,8},{10,11... | collective-permute-start | bytes 2064392 | tf_op jit(solution)/shard_map/ppermute | solution.py:16
  132.4 16.2 %collective-permute-start.31 = (bf16[3,64,1792]{2,1,0:T(8,128)(2,1)S(1)}, bf16[3,64,1792]{2,1,0:T(8,128)(2,1)S(1)}, u32[]{:S(2)}, u32[]{:S(2)}) collective-permute-start(bf16[3,64,1792]{2,1,0:T(8,128)(2,1)S(1)} %pad_maximum_fusion.23), channel_id=1, source_target_pairs={{0,64},{32,96},{64,0},{96,32},{1,65},{33,97},{65,1},{97,33},{2,66}... | collective-permute-start | bytes 2064392 | tf_op jit(solution)/shard_map/ppermute | solution.py:16
  149.6 25.6 %copy-start.5 = (bf16[1792,1024]{1,0:T(8,128)(2,1)S(1)}, bf16[1792,1024]{1,0:T(8,128)(2,1)}, u32[]{:S(2)}) copy-start(bf16[1792,1024]{1,0:T(8,128)(2,1)} %copy-done.4) | copy-start | bytes 11010052
  149.7 41.2 %collective-permute-start.24 = (bf16[2,128,1792]{2,1,0:T(8,128)(2,1)S(1)}, bf16[2,128,1792]{2,1,0:T(8,128)(2,1)S(1)}, u32[]{:S(2)}, u32[]{:S(2)}) collective-permute-start(bf16[2,128,1792]{2,1,0:T(8,128)(2,1)S(1)} %slice.284), channel_id=1, source_target_pairs={{0,1},{1,0},{2,3},{3,2},{4,5},{5,4},{6,7},{7,6},{8,9},{9,8},{10,11... | collective-permute-start | bytes 2752520 | tf_op jit(solution)/shard_map/ppermute | solution.py:16
  152.7 38.1 %collective-permute-start.32 = (bf16[2,128,1792]{2,1,0:T(8,128)(2,1)S(1)}, bf16[2,128,1792]{2,1,0:T(8,128)(2,1)S(1)}, u32[]{:S(2)}, u32[]{:S(2)}) collective-permute-start(bf16[2,128,1792]{2,1,0:T(8,128)(2,1)S(1)} %slice.289), channel_id=1, source_target_pairs={{0,3},{1,2},{2,1},{3,0},{4,7},{5,6},{6,5},{7,4},{8,11},{9,10},{10,... | collective-permute-start | bytes 2752520 | tf_op jit(solution)/shard_map/ppermute | solution.py:16
  152.7 38.1 %collective-permute-start.40 = (bf16[2,128,1792]{2,1,0:T(8,128)(2,1)S(1)}, bf16[2,128,1792]{2,1,0:T(8,128)(2,1)S(1)}, u32[]{:S(2)}, u32[]{:S(2)}) collective-permute-start(bf16[2,128,1792]{2,1,0:T(8,128)(2,1)S(1)} %slice.294), channel_id=1, source_target_pairs={{0,64},{32,96},{64,0},{96,32},{1,65},{33,97},{65,1},{97,33},{2,66}... | collective-permute-start | bytes 2752520 | tf_op jit(solution)/shard_map/ppermute | solution.py:16
  152.7 20.2 %collective-permute-start.43 = (bf16[1,128,1792]{2,1,0:T(8,128)(2,1)S(1)}, bf16[1,128,1792]{2,1,0:T(8,128)(2,1)S(1)}, u32[]{:S(2)}, u32[]{:S(2)}) collective-permute-start(bf16[1,128,1792]{2,1,0:T(8,128)(2,1)S(1)} %get-tuple-element.270), channel_id=1, source_target_pairs={{0,64},{32,96},{64,0},{96,32},{1,65},{33,97},{65,1},{97,33},{2,66}... | collective-permute-start | bytes 1376264 | tf_op jit(solution)/shard_map/ppermute | solution.py:16
  154.8 21.6 %collective-permute-start.42 = (bf16[1,128,1792]{2,1,0:T(8,128)(2,1)S(1)}, bf16[1,128,1792]{2,1,0:T(8,128)(2,1)S(1)}, u32[]{:S(2)}, u32[]{:S(2)}) collective-permute-start(bf16[1,128,1792]{2,1,0:T(8,128)(2,1)S(1)} %get-tuple-element.268), channel_id=1, source_target_pairs={{0,3},{1,2},{2,1},{3,0},{4,7},{5,6},{6,5},{7,4},{8,11},{9,10},{10,... | collective-permute-start | bytes 1376264 | tf_op jit(solution)/shard_map/ppermute | solution.py:16
  173.0 8.5 %collective-permute-start.41 = (bf16[1,128,1792]{2,1,0:T(8,128)(2,1)S(1)}, bf16[1,128,1792]{2,1,0:T(8,128)(2,1)S(1)}, u32[]{:S(2)}, u32[]{:S(2)}) collective-permute-start(bf16[1,128,1792]{2,1,0:T(8,128)(2,1)S(1)} %get-tuple-element.266), channel_id=1, source_target_pairs={{0,1},{1,0},{2,3},{3,2},{4,5},{5,4},{6,7},{7,6},{8,9},{9,8},{10,11... | collective-permute-start | bytes 1376264 | tf_op jit(solution)/shard_map/ppermute | solution.py:16
  182.8 5.7 %collective-permute-start.44 = (bf16[3,32,1024]{2,1,0:T(8,128)(2,1)S(1)}, bf16[3,32,1024]{2,1,0:T(8,128)(2,1)S(1)}, u32[]{:S(2)}, u32[]{:S(2)}) collective-permute-start(bf16[3,32,1024]{2,1,0:T(8,128)(2,1)S(1)} %get-tuple-element.264), channel_id=1, source_target_pairs={{0,4},{4,0},{8,12},{12,8},{16,20},{20,16},{24,28},{28,24},{1,5},{5... | collective-permute-start | bytes 589832 | tf_op jit(solution)/shard_map/ppermute | solution.py:16
  183.6 7.3 %collective-permute-start.45 = (bf16[3,32,1024]{2,1,0:T(8,128)(2,1)S(1)}, bf16[3,32,1024]{2,1,0:T(8,128)(2,1)S(1)}, u32[]{:S(2)}, u32[]{:S(2)}) collective-permute-start(bf16[3,32,1024]{2,1,0:T(8,128)(2,1)S(1)} %get-tuple-element.263), channel_id=1, source_target_pairs={{0,12},{4,8},{8,4},{12,0},{16,28},{20,24},{24,20},{28,16},{1,13},{... | collective-permute-start | bytes 589832 | tf_op jit(solution)/shard_map/ppermute | solution.py:16
  202.0 10.0 %collective-permute-start.46 = (bf16[3,32,1024]{2,1,0:T(8,128)(2,1)S(1)}, bf16[3,32,1024]{2,1,0:T(8,128)(2,1)S(1)}, u32[]{:S(2)}, u32[]{:S(2)}) collective-permute-start(bf16[3,32,1024]{2,1,0:T(8,128)(2,1)S(1)} %get-tuple-element.262), channel_id=1, source_target_pairs={{0,4},{4,0},{8,12},{12,8},{16,20},{20,16},{24,28},{28,24},{1,5},{5... | collective-permute-start | bytes 589832 | tf_op jit(solution)/shard_map/ppermute | solution.py:16
  202.2 10.4 %collective-permute-start.47 = (bf16[3,32,1024]{2,1,0:T(8,128)(2,1)S(1)}, bf16[3,32,1024]{2,1,0:T(8,128)(2,1)S(1)}, u32[]{:S(2)}, u32[]{:S(2)}) collective-permute-start(bf16[3,32,1024]{2,1,0:T(8,128)(2,1)S(1)} %get-tuple-element.261), channel_id=1, source_target_pairs={{0,12},{4,8},{8,4},{12,0},{16,28},{20,24},{24,20},{28,16},{1,13},{... | collective-permute-start | bytes 589832 | tf_op jit(solution)/shard_map/ppermute | solution.py:16
  203.6 9.0 %collective-permute-start.48 = (bf16[3,64,1024]{2,1,0:T(8,128)(2,1)S(1)}, bf16[3,64,1024]{2,1,0:T(8,128)(2,1)S(1)}, u32[]{:S(2)}, u32[]{:S(2)}) collective-permute-start(bf16[3,64,1024]{2,1,0:T(8,128)(2,1)S(1)} %get-tuple-element.202), channel_id=1, source_target_pairs={{0,4},{4,0},{8,12},{12,8},{16,20},{20,16},{24,28},{28,24},{1,5},{5... | collective-permute-start | bytes 1179656 | tf_op jit(solution)/shard_map/ppermute | solution.py:16
  205.0 9.0 %collective-permute-start.49 = (bf16[3,64,1024]{2,1,0:T(8,128)(2,1)S(1)}, bf16[3,64,1024]{2,1,0:T(8,128)(2,1)S(1)}, u32[]{:S(2)}, u32[]{:S(2)}) collective-permute-start(bf16[3,64,1024]{2,1,0:T(8,128)(2,1)S(1)} %get-tuple-element.203), channel_id=1, source_target_pairs={{0,12},{4,8},{8,4},{12,0},{16,28},{20,24},{24,20},{28,16},{1,13},{... | collective-permute-start | bytes 1179656 | tf_op jit(solution)/shard_map/ppermute | solution.py:16
  207.0 6.9 %collective-permute-start.50 = (bf16[1792,512]{1,0:T(8,128)(2,1)S(1)}, bf16[1792,512]{1,0:T(8,128)(2,1)S(1)}, u32[]{:S(2)}, u32[]{:S(2)}) collective-permute-start(bf16[1792,512]{1,0:T(8,128)(2,1)S(1)} %convolution_convert_fusion.2), channel_id=1, source_target_pairs={{0,32},{32,0},{64,96},{96,64},{1,33},{33,1},{65,97},{97,65},{2,34}... | collective-permute-start | bytes 5505032 | tf_op jit(solution)/shard_map/ppermute | solution.py:16
  212.0 19.7 %collective-permute-start.54 = (bf16[512,1792]{1,0:T(8,128)(2,1)S(1)}, bf16[512,1792]{1,0:T(8,128)(2,1)S(1)}, u32[]{:S(2)}, u32[]{:S(2)}) collective-permute-start(bf16[512,1792]{1,0:T(8,128)(2,1)S(1)} %convolution_convert_fusion), channel_id=1, source_target_pairs={{0,32},{32,0},{64,96},{96,64},{1,33},{33,1},{65,97},{97,65},{2,34}... | collective-permute-start | bytes 5505032 | tf_op jit(solution)/shard_map/ppermute | solution.py:16
  214.0 17.7 %collective-permute-start.53 = (bf16[512,1792]{1,0:T(8,128)(2,1)S(1)}, bf16[512,1792]{1,0:T(8,128)(2,1)S(1)}, u32[]{:S(2)}, u32[]{:S(2)}) collective-permute-start(bf16[512,1792]{1,0:T(8,128)(2,1)S(1)} %convolution_convert_fusion.1), channel_id=1, source_target_pairs={{0,32},{32,0},{64,96},{96,64},{1,33},{33,1},{65,97},{97,65},{2,34}... | collective-permute-start | bytes 5505032 | tf_op jit(solution)/shard_map/ppermute | solution.py:16
  214.4 5.7 %collective-permute-start.55 = (bf16[3,16,1024]{2,1,0:T(8,128)(2,1)S(1)}, bf16[3,16,1024]{2,1,0:T(8,128)(2,1)S(1)}, u32[]{:S(2)}, u32[]{:S(2)}) collective-permute-start(bf16[3,16,1024]{2,1,0:T(8,128)(2,1)S(1)} %constant_dynamic-slice_fusion.5), channel_id=1, source_target_pairs={{0,64},{32,96},{64,0},{96,32},{1,65},{33,97},{65,1},{97,33},{2,66}... | collective-permute-start | bytes 294920 | tf_op jit(solution)/shard_map/ppermute | solution.py:16
  214.8 7.6 %collective-permute-start.56 = (bf16[3,16,1024]{2,1,0:T(8,128)(2,1)S(1)}, bf16[3,16,1024]{2,1,0:T(8,128)(2,1)S(1)}, u32[]{:S(2)}, u32[]{:S(2)}) collective-permute-start(bf16[3,16,1024]{2,1,0:T(8,128)(2,1)S(1)} %get-tuple-element.218), channel_id=1, source_target_pairs={{0,16},{4,20},{8,24},{12,28},{16,0},{20,4},{24,8},{28,12},{1,17},{... | collective-permute-start | bytes 294920 | tf_op jit(solution)/shard_map/ppermute | solution.py:16
  217.3 11.0 %collective-permute-start.51 = (bf16[3,64,1024]{2,1,0:T(8,128)(2,1)S(1)}, bf16[3,64,1024]{2,1,0:T(8,128)(2,1)S(1)}, u32[]{:S(2)}, u32[]{:S(2)}) collective-permute-start(bf16[3,64,1024]{2,1,0:T(8,128)(2,1)S(1)} %get-tuple-element.209), channel_id=1, source_target_pairs={{0,4},{4,0},{8,12},{12,8},{16,20},{20,16},{24,28},{28,24},{1,5},{5... | collective-permute-start | bytes 1179656 | tf_op jit(solution)/shard_map/ppermute | solution.py:16
  220.1 11.6 %collective-permute-start.52 = (bf16[3,64,1024]{2,1,0:T(8,128)(2,1)S(1)}, bf16[3,64,1024]{2,1,0:T(8,128)(2,1)S(1)}, u32[]{:S(2)}, u32[]{:S(2)}) collective-permute-start(bf16[3,64,1024]{2,1,0:T(8,128)(2,1)S(1)} %get-tuple-element.210), channel_id=1, source_target_pairs={{0,12},{4,8},{8,4},{12,0},{16,28},{20,24},{24,20},{28,16},{1,13},{... | collective-permute-start | bytes 1179656 | tf_op jit(solution)/shard_map/ppermute | solution.py:16
  222.4 5.8 %collective-permute-start.57 = (bf16[3,16,1024]{2,1,0:T(8,128)(2,1)S(1)}, bf16[3,16,1024]{2,1,0:T(8,128)(2,1)S(1)}, u32[]{:S(2)}, u32[]{:S(2)}) collective-permute-start(bf16[3,16,1024]{2,1,0:T(8,128)(2,1)S(1)} %get-tuple-element.219), channel_id=1, source_target_pairs={{0,80},{4,84},{8,88},{12,92},{16,64},{20,68},{24,72},{28,76},{32,1... | collective-permute-start | bytes 294920 | tf_op jit(solution)/shard_map/ppermute | solution.py:32
  232.0 11.4 %collective-permute-start.58 = (bf16[3,16,1024]{2,1,0:T(8,128)(2,1)S(1)}, bf16[3,16,1024]{2,1,0:T(8,128)(2,1)S(1)}, u32[]{:S(2)}, u32[]{:S(2)}) collective-permute-start(bf16[3,16,1024]{2,1,0:T(8,128)(2,1)S(1)} %constant_dynamic-slice_fusion.2), channel_id=1, source_target_pairs={{0,64},{32,96},{64,0},{96,32},{1,65},{33,97},{65,1},{97,33},{2,66}... | collective-permute-start | bytes 294920 | tf_op jit(solution)/shard_map/ppermute | solution.py:16
  232.4 11.0 %collective-permute-start.59 = (bf16[3,16,1024]{2,1,0:T(8,128)(2,1)S(1)}, bf16[3,16,1024]{2,1,0:T(8,128)(2,1)S(1)}, u32[]{:S(2)}, u32[]{:S(2)}) collective-permute-start(bf16[3,16,1024]{2,1,0:T(8,128)(2,1)S(1)} %get-tuple-element.226), channel_id=1, source_target_pairs={{0,16},{4,20},{8,24},{12,28},{16,0},{20,4},{24,8},{28,12},{1,17},{... | collective-permute-start | bytes 294920 | tf_op jit(solution)/shard_map/ppermute | solution.py:16
  234.7 8.7 %collective-permute-start.60 = (bf16[3,16,1024]{2,1,0:T(8,128)(2,1)S(1)}, bf16[3,16,1024]{2,1,0:T(8,128)(2,1)S(1)}, u32[]{:S(2)}, u32[]{:S(2)}) collective-permute-start(bf16[3,16,1024]{2,1,0:T(8,128)(2,1)S(1)} %get-tuple-element.227), channel_id=1, source_target_pairs={{0,80},{4,84},{8,88},{12,92},{16,64},{20,68},{24,72},{28,76},{32,1... | collective-permute-start | bytes 294920 | tf_op jit(solution)/shard_map/ppermute | solution.py:32
  (11 other events, 85.1 us)
